TPU v7x, 512 devices: a whole 4x8x8 slice. The times are simulated.
512 devices in a mesh: branch: 16 (over y_lo, z), seq: 32 (over x, y_hi, core).
Axes of the slice: x: 4, y: 8 (y_hi: 4, y_lo: 2; y = y_hi * 2 + y_lo), z: 8, core: 2. Of those that a mesh axis runs over, the one named last changes fastest.
Arguments:
- queries: bfloat16 [64, 4096], P('branch', 'seq'), may hold values from -16 to 16
- row_branch: int32 [64], replicated, may hold values from 0 to 15, as said below
- suffix_len: int32 [64], P('branch'), may hold values from 1 to 2048, as said below
- common_keys: bfloat16 [131072, 512], P(('branch', 'seq')), may hold values from -16 to 16
- common_values: bfloat16 [131072, 512], P(('branch', 'seq')), may hold values from -6 to 6
- branch_keys: bfloat16 [16, 16384, 512], P('branch', 'seq'), may hold values from -6 to 6
- branch_values: bfloat16 [16, 16384, 512], P('branch', 'seq'), may hold values from -6 to 6
- suffix_keys: bfloat16 [64, 2048, 512], P('branch', 'seq'), may hold values from -6 to 6
- suffix_values: bfloat16 [64, 2048, 512], P('branch', 'seq'), may hold values from -6 to 6
Outputs:
- attended: bfloat16 [64, 4096], P('branch', 'seq')
Inputs may be any that keep to these rules, and one draw needn't show every extreme that they name: `row_branch`: each of the 16 branches is named by exactly 4 rows. `suffix_len`: some row has all 2048 suffix tokens live.
All inputs are finite; a program needn't handle non-finite values.
Results may differ from a plain program's by a relative error of at most 0.0029.
Values may be sent and summed in bfloat16 or wider, within the bound.
No kernel may reach another device: no remote copies, remote signals or barrier semaphores. Data moves between devices by JAX's collectives and lax.ppermute only.
A program may use at most 64 MiB of HBM per device.

v0:
```python
import math

import jax
import jax.numpy as jnp
from jax import lax
from jax.sharding import PartitionSpec as P

HEADS = 32
KV_HEADS = 4
HEAD_DIM = 128


NEG_BIG = -1e30


def local(
    queries,
    row_branch,
    suffix_len,
    common_keys,
    common_values,
    branch_keys,
    branch_values,
    suffix_keys,
    suffix_values,
):
    seq_count = lax.axis_size("seq")
    branch_count = lax.axis_size("branch")
    branch_at = lax.axis_index("branch")
    seq_at = lax.axis_index("seq")
    own_rows = queries.shape[0]
    row_count = row_branch.shape[0]
    per_kv = HEADS // KV_HEADS
    heads_here = HEADS // seq_count
    col_width = heads_here * HEAD_DIM
    first_row = branch_at * own_rows
    score_scale = 1.0 / math.sqrt(HEAD_DIM)
    slots_here = suffix_keys.shape[1]
    group_q = lax.all_gather(queries, "seq", axis=1, tiled=True)
    all_q = lax.all_gather(group_q, "branch", axis=0, tiled=True)
    query_all = all_q.reshape(row_count, KV_HEADS, per_kv, HEAD_DIM)
    query_own = group_q.reshape(own_rows, KV_HEADS, per_kv, HEAD_DIM)
    in_branch = (row_branch == branch_at).astype(jnp.int32)
    rank_in = jnp.cumsum(in_branch) - 1
    select = (in_branch[None, :] == 1) & (
        rank_in[None, :] == jnp.arange(own_rows, dtype=jnp.int32)[:, None]
    )
    select_f = select.astype(jnp.float32)
    branch_q = jnp.dot(
        select.astype(jnp.bfloat16), all_q, preferred_element_type=jnp.float32
    ).astype(jnp.bfloat16)
    branch_q = branch_q.reshape(own_rows, KV_HEADS, per_kv, HEAD_DIM)
    key_suffix = suffix_keys.reshape(own_rows, slots_here, KV_HEADS, HEAD_DIM)
    val_suffix = suffix_values.reshape(own_rows, slots_here, KV_HEADS, HEAD_DIM)
    suffix_scores = (
        jnp.einsum("rkgd,rtkd->rkgt", query_own, key_suffix, preferred_element_type=jnp.float32)
        * score_scale
    )
    positions = seq_at * slots_here + jnp.arange(slots_here, dtype=jnp.int32)
    is_live = positions[None, :] < suffix_len[:, None]
    suffix_masked = jnp.where(is_live[:, None, None, :], suffix_scores, NEG_BIG)
    key_common = common_keys.reshape(-1, KV_HEADS, HEAD_DIM)
    key_branch = branch_keys.reshape(-1, KV_HEADS, HEAD_DIM)
    common_scores = (
        jnp.einsum("rkgd,tkd->rkgt", query_all, key_common, preferred_element_type=jnp.float32)
        * score_scale
    )
    branch_scores = (
        jnp.einsum("rkgd,tkd->rkgt", branch_q, key_branch, preferred_element_type=jnp.float32)
        * score_scale
    )
    local_max = jnp.max(common_scores, axis=-1)
    branch_max = jnp.max(branch_scores, axis=-1)
    placed = jnp.max(jnp.where(select[:, :, None, None], branch_max[:, None], NEG_BIG), axis=0)
    local_max = jnp.maximum(local_max, placed)
    own_max = jnp.maximum(
        lax.dynamic_slice_in_dim(local_max, first_row, own_rows, 0), jnp.max(suffix_masked, axis=-1)
    )
    local_max = lax.dynamic_update_slice_in_dim(local_max, own_max, first_row, 0)
    row_max = lax.pmax(local_max, ("branch", "seq"))
    branch_rmax = jnp.dot(
        select_f, row_max.reshape(row_count, HEADS), precision=lax.Precision.HIGHEST
    )
    suffix_rmax = lax.dynamic_slice_in_dim(row_max, first_row, own_rows, 0)
    val_common = common_values.reshape(-1, KV_HEADS, HEAD_DIM)
    val_branch = branch_values.reshape(-1, KV_HEADS, HEAD_DIM)
    common_w = jnp.exp(common_scores - row_max[..., None])
    sum_term = jnp.sum(common_w, axis=-1).reshape(row_count, HEADS)
    out_term = jnp.einsum(
        "rkgt,tkd->rkgd",
        common_w.astype(jnp.bfloat16),
        val_common,
        preferred_element_type=jnp.float32,
    )
    out_term = out_term.reshape(row_count, HEADS * HEAD_DIM)
    branch_w = jnp.exp(branch_scores - branch_rmax.reshape(own_rows, KV_HEADS, per_kv)[..., None])
    branch_sum = jnp.sum(branch_w, axis=-1).reshape(own_rows, HEADS)
    branch_out = jnp.einsum(
        "rkgt,tkd->rkgd",
        branch_w.astype(jnp.bfloat16),
        val_branch,
        preferred_element_type=jnp.float32,
    )
    branch_out = branch_out.reshape(own_rows, HEADS * HEAD_DIM)
    sum_term = sum_term + jnp.dot(select_f.T, branch_sum, precision=lax.Precision.HIGHEST)
    out_term = out_term + jnp.dot(select_f.T, branch_out, precision=lax.Precision.HIGHEST)
    out_flat = out_term.reshape(branch_count, own_rows, seq_count, col_width).transpose(0, 2, 1, 3)
    out_flat = out_flat.reshape(branch_count * seq_count * own_rows, col_width)
    sum_flat = sum_term.reshape(branch_count, own_rows, seq_count, heads_here).transpose(0, 2, 1, 3)
    sum_flat = sum_flat.reshape(branch_count * seq_count * own_rows, heads_here)
    numer_own, total_own = (
        lax.psum_scatter(out_flat, ("branch", "seq"), scatter_dimension=0, tiled=True),
        lax.psum_scatter(sum_flat, ("branch", "seq"), scatter_dimension=0, tiled=True),
    )
    suffix_w = jnp.where(
        is_live[:, None, None, :], jnp.exp(suffix_masked - suffix_rmax[..., None]), 0.0
    )
    suffix_sum = jnp.sum(suffix_w, axis=-1).reshape(own_rows, HEADS)
    suffix_out = jnp.einsum(
        "rkgt,rtkd->rkgd",
        suffix_w.astype(jnp.bfloat16),
        val_suffix,
        preferred_element_type=jnp.float32,
    )
    suffix_out = suffix_out.reshape(own_rows, HEADS * HEAD_DIM)
    suffix_numer, suffix_total = (
        lax.psum_scatter(suffix_out, "seq", scatter_dimension=1, tiled=True),
        lax.psum_scatter(suffix_sum, "seq", scatter_dimension=1, tiled=True),
    )
    numer_own = numer_own + suffix_numer
    total_own = total_own + suffix_total
    attended = numer_own.reshape(own_rows, heads_here, HEAD_DIM) / total_own[:, :, None]
    return attended.reshape(own_rows, col_width).astype(jnp.bfloat16)


def solution(mesh):
    return jax.shard_map(
        local,
        mesh=mesh,
        in_specs=(
            P("branch", "seq"),
            P(),
            P("branch"),
            P(("branch", "seq"), None),
            P(("branch", "seq"), None),
            P("branch", "seq", None),
            P("branch", "seq", None),
            P("branch", "seq", None),
            P("branch", "seq", None),
        ),
        out_specs=P("branch", "seq"),
        check_vma=False,
    )
```

profile of v0, /device:TPU:1, one launch (start us, length us, event | category | flops | bytes accessed | tf_op | source)
XLA Modules:
  0.0 480.4 jit_solution(4944735867009745510)
XLA Ops:
  7.4 47.0 %all_gather.6 = bf16[4,4096]{1,0:T(4,128)(2,1)S(1)} all-gather(bf16[4,128]{1,0:T(4,128)(2,1)} %param.9), channel_id=1, replica_groups=mesh['branch'=16,'seq'=32] {'seq'}, dimensions={1}, use_global_device_ids=true | all-gather | bytes 33792 | tf_op jit(solution)/shard_map/all_gather | solution.py:39
  54.4 34.2 %all-gather = bf16[16,4,4096]{2,1,0:T(4,128)(2,1)S(1)} all-gather(bf16[1,4,4096]{2,1,0:T(4,128)(2,1)S(1)} %bitcast.112), channel_id=1, replica_groups=mesh['branch'=16,'seq'=32] {'branch'}, dimensions={0}, use_global_device_ids=true | all-gather | bytes 557056 | tf_op jit(solution)/shard_map/all_gather | solution.py:40
  88.6 0.1 reshape.186
  88.7 0.5 reshape.164
  89.3 0.1 copy.101
  89.4 0.1 reduce-window.8
  89.5 0.1 add_reduce_fusion
  89.6 0.1 reshape.167
  89.8 0.2 fusion.6
  89.9 1.0 fusion.45
  90.9 0.1 select_reduce_fusion
  91.0 0.1 reshape.163
  91.1 0.1 broadcast_compare_fusion
  91.2 0.3 fusion.46
  91.5 0.1 copy.106
  91.6 0.6 bitcast_reduce_fusion
  92.2 0.1 dynamic-slice_maximum_fusion
  92.3 0.2 dynamic_update_slice.3
  92.5 101.5 %pmax.7 = f32[64,4,8]{0,2,1:T(8,128)S(1)} all-reduce(f32[64,4,8]{0,2,1:T(8,128)S(1)} %dynamic_update_slice.3), channel_id=1, replica_groups=mesh['branch'=16,'seq'=32] {'branch','seq'}, use_global_device_ids=true, to_apply=%region_5.6 | all-reduce | flops 2048 | bytes 16384 | tf_op jit(solution)/shard_map/pmax | solution.py:80
  194.0 0.1 constant_dynamic-slice_fusion.2
  194.0 0.1 copy.113
  194.1 0.2 fusion.12
  194.4 2.0 copy.136
  196.5 0.2 fusion.34
  196.7 0.8 fusion.1
  197.5 1.2 reshape.174
  198.7 1.2 convolution_bitcast_fusion.1
  199.9 0.1 reshape.170
  200.0 0.7 convolution_bitcast_fusion
  200.7 0.1 copy.109
  200.8 1.1 fusion.3
  202.0 0.2 copy.143
  202.2 1.7 copy.112
  203.9 0.2 fusion.19
  204.1 0.1 reshape.181
  204.2 0.2 convolution_add_fusion.1
  204.4 0.1 copy.116
  204.5 0.2 copy.117
  204.7 0.2 reshape.183
  204.9 0.2 fusion.25
  205.0 0.1 copy.131
  205.1 1.3 dynamic-slice.2
  206.4 134.8 %all-reduce.2 = f32[4,32]{0,1:T(8,128)S(1)} all-reduce(f32[4,32]{0,1:T(8,128)S(1)} %bitcast.117), channel_id=5, replica_groups=mesh['branch'=16,'seq'=32] {'seq'}, use_global_device_ids=true, to_apply=%region_12.13.clone | all-reduce | flops 128 | bytes 1024
  341.2 100.3 %all-reduce.1 = f32[2048,1]{0,1:T(1,128)S(1)} all-reduce(f32[2048,1]{0,1:T(1,128)S(1)} %reshape.183), channel_id=4, replica_groups=mesh['branch'=16,'seq'=32] {'branch','seq'}, use_global_device_ids=true, to_apply=%region_10.11.clone | all-reduce | flops 2048 | bytes 16384
  441.5 0.7 fusion.41
  442.2 0.9 copy.133
  443.1 28.5 %all-reduce.5.cloned.1.call-done = f32[2048,128]{1,0:T(8,128)} async-done(((f32[2048,128]{1,0:T(8,128)}), f32[2048,128]{1,0:T(8,128)}) %all-reduce.5.cloned.1.call-update) | async-done | bytes 1048592
  471.6 1.3 fusion.38
  (28 shorter events, 0.2 us)
Async XLA Ops:
  7.4 186.8 %copy-start = (bf16[4,64,512]{2,1,0:T(8,128)(2,1)S(1)}, bf16[4,64,512]{2,1,0:T(8,128)(2,1)}, u32[]{:S(2)}) copy-start(bf16[4,64,512]{2,1,0:T(8,128)(2,1)} %param.17) | copy-start | bytes 786436
  7.4 81.9 %copy-start.6 = (s32[64]{0:T(128)S(1)}, s32[64]{0:T(128)}, u32[]{:S(2)}) copy-start(s32[64]{0:T(128)} %param.10) | copy-start | bytes 772
  7.4 82.2 %copy-start.2 = (bf16[1,512,512]{2,1,0:T(8,128)(2,1)S(1)}, bf16[1,512,512]{2,1,0:T(8,128)(2,1)}, u32[]{:S(2)}) copy-start(bf16[1,512,512]{2,1,0:T(8,128)(2,1)} %param.14) | copy-start | bytes 1572868
  7.4 434.8 %reduce-scatter.5.cloned.1.call-start = ((), (), s32[]{:S(2)}) async-start(), calls=%async_computation.1 | async-start | bytes 2162688
  88.7 2.3 copy-start.3
  88.7 2.4 copy-start.7
  88.7 2.5 copy-start.4
  196.4 275.2 %all-reduce.5.cloned.1.call-start = ((), (), s32[]{:S(2)}) async-start(), calls=%async_computation.2 | async-start | bytes 2097152
  197.4 2.5 copy-start.5
  202.2 1.7 copy-start.1
Sparse Core Ops, SparseCore 0:
  196.5 90.1 reduce-scatter.4
Sparse Core Ops, SparseCore 1:
  204.0 267.6 all-reduce.4
where the time goes:
time: 481 us; the launch traced here: 480 us
  blocking collectives  418 us (87%)
  waiting for transfers between devices  28.5 us (6%)
  between operations  15.1 us (3%)
  local copies, waits for them, and re-layouts  9.54 us (2%)
  matrix products  5.72 us (1%)
    unnamed x2, blocking collectives  235 us
    pmax x1, blocking collectives, local(): row_max = lax.pmax(local_max, ('branch', 'seq'))  101 us
    all_gather x1, blocking collectives, local(): group_q = lax.all_gather(queries, 'seq', axis=1, tiled=True)  47 us
    all_gather x1, blocking collectives, local(): all_q = lax.all_gather(group_q, 'branch', axis=0, tiled=True)  34.2 us
    unnamed x4, waiting for transfers between devices  28.5 us
  transfers between devices with their start and end apart: 2, of which 1 were waited for; matrix products, arithmetic and copies ran while one was open for 2% of the time, Pallas kernels for 0%

commit v1 on v0

v1 whole, which is shorter than its diff:
```python
import functools
import math

import jax
import jax.numpy as jnp
from jax import lax
from jax.experimental import pallas as pl
from jax.experimental.pallas import tpu as pltpu
from jax.sharding import Mesh
from jax.sharding import PartitionSpec as P

HEADS = 32
KV_HEADS = 4
GROUP = HEADS // KV_HEADS
HEAD_DIM = 128
N_X, N_YHI, N_CORE, N_YLO, N_Z = 4, 4, 2, 2, 8
PLANE = ("z", "yhi", "ylo", "core")
PEERS = N_Z * N_YHI * N_YLO * N_CORE
ROWS = 64
OWN = 4
COM, BRA, SUF = 256, 512, 64
KEYS = COM + BRA + OWN * SUF
LINES = PEERS * OWN
PICKED = OWN * GROUP
CHUNK = OWN + 1
LOW = -1e30
F32 = jnp.float32
BF16 = jnp.bfloat16
SCALE = math.log2(math.e) / math.sqrt(HEAD_DIM)
VMEM = pl.BlockSpec(memory_space=pltpu.VMEM)
SMEM = pl.BlockSpec(memory_space=pltpu.SMEM)
ANY = pl.BlockSpec(memory_space=pl.ANY)
VMEM_LIMIT = 48 * 1024 * 1024


def pack_kernel(place, ck, cv, bk, bv, sk, sv, *rest):
    outs, sem = rest[:N_X], rest[N_X]
    x = place[1]
    copies = []
    for i in range(N_X):
        head = lax.rem(x + i, N_X)
        cols = pl.ds(pl.multiple_of(head * HEAD_DIM, HEAD_DIM), HEAD_DIM)
        at = 0
        for n, (src, count) in enumerate(
            ((ck, COM), (bk, BRA), (sk, OWN * SUF), (cv, COM), (bv, BRA), (sv, OWN * SUF))
        ):
            copy = pltpu.make_async_copy(src.at[:, cols], outs[i].at[pl.ds(at, count)], sem.at[i, n])
            copy.start()
            copies.append(copy)
            at += count
    for copy in copies:
        copy.wait()


def attend(q, keys, values, mask=None):
    scores = []
    for i, key in enumerate(keys):
        s = lax.dot_general(q, key, (((1,), (1,)), ((), ())), preferred_element_type=F32) * SCALE
        scores.append(s if mask is None else jnp.where(mask[i], s, LOW))
    top = jnp.max(functools.reduce(jnp.maximum, scores), axis=1, keepdims=True)
    total = out = None
    for i, (s, value) in enumerate(zip(scores, values)):
        w = jnp.exp2(s - top)
        if mask is not None:
            w = jnp.where(mask[i], w, 0.0)
        o = jnp.dot(w.astype(BF16), value, preferred_element_type=F32)
        total = w if total is None else total + w
        out = o if out is None else out + o
    return out, top, jnp.sum(total, axis=1, keepdims=True)


def attend_kernel(place, row_branch, suffix_len, q_ref, kv0, kv1, kv2, kv3, out_ref, pick):
    branch, x, yhi, core = place[0], place[1], place[2], place[3]
    kvs = (kv0, kv1, kv2, kv3)

    def blocks(at, count):
        return [kv[pl.ds(at, count)] for kv in kvs], [kv[pl.ds(KEYS + at, count)] for kv in kvs]

    found = jnp.int32(0)
    for i in range(ROWS):
        pick[found] = jnp.int32(i)
        found = found + (row_branch[i] == branch).astype(jnp.int32)

    q = q_ref[...]
    out, top, total = attend(q, *blocks(0, COM))

    def lines(shape, axis):
        at = lax.broadcasted_iota(jnp.int32, shape, axis)
        slot = (at >> 3) & (OWN - 1)
        row = jnp.zeros(shape, jnp.int32)
        for j in range(OWN):
            row = jnp.where(slot == j, jnp.where(at < PICKED, pick[j], branch * OWN + j), row)
        ylo, z, r = row >> 5, (row >> 2) & 7, row & 3
        yh, co = (at >> 1) & 3, at & 1
        return (((z * N_YHI + yh) * N_YLO + ylo) * N_CORE + co) * OWN + r

    shape = (2 * PICKED, LINES)
    select = lax.broadcasted_iota(jnp.int32, shape, 1) == lines(shape, 0)
    q_sel = jnp.dot(select.astype(F32).astype(BF16), q, preferred_element_type=F32).astype(BF16)
    b_out, b_top, b_total = attend(q_sel[:PICKED], *blocks(COM, BRA))

    shape = (PICKED, OWN * SUF)
    q_row = lax.broadcasted_iota(jnp.int32, shape, 0) >> 3
    slot = lax.broadcasted_iota(jnp.int32, shape, 1)
    k_row, slot = slot >> 6, slot & (SUF - 1)
    live = jnp.zeros(shape, jnp.int32)
    for j in range(OWN):
        live = jnp.where(k_row == j, suffix_len[j], live)
    mask = []
    for i in range(N_X):
        from_x = lax.rem(x + N_X - i, N_X)
        first = ((from_x * N_YHI + yhi) * N_CORE + core) * SUF
        mask.append((q_row == k_row) & (slot + first < live))
    s_out, s_top, s_total = attend(q_sel[PICKED:], *blocks(COM + BRA, OWN * SUF), mask)

    square = (2 * PICKED, 2 * PICKED)
    eye = lax.broadcasted_iota(jnp.int32, square, 0) == lax.broadcasted_iota(jnp.int32, square, 1)

    def across(a, b):
        col = jnp.broadcast_to(jnp.concatenate([a, b], axis=0), square)
        return jnp.sum(jnp.where(eye, col, 0.0), axis=0, keepdims=True)

    shape = (LINES, 2 * PICKED)
    place_of = lax.broadcasted_iota(jnp.int32, shape, 0) == lines(shape, 1)
    p_top = jnp.where(place_of, jnp.broadcast_to(across(b_top, s_top), shape), LOW)
    high = jnp.maximum(top, jnp.max(p_top, axis=1, keepdims=True))
    weight = jnp.where(place_of, jnp.exp2(p_top - high), 0.0)
    scale = jnp.exp2(top - high)
    parts = jnp.concatenate([b_out, s_out], axis=0)
    out = out * scale + jnp.dot(
        weight, parts, precision=lax.Precision.HIGHEST, preferred_element_type=F32
    )
    total = total * scale + jnp.sum(weight * across(b_total, s_total), axis=1, keepdims=True)

    shape = (LINES, HEAD_DIM)
    lane = lax.broadcasted_iota(jnp.int32, shape, 1)
    r = lax.broadcasted_iota(jnp.int32, shape, 0) & (OWN - 1)
    stat = jnp.where(lane == r, high, 0.0) + jnp.where(lane == r + OWN, total, 0.0)
    stat = sum(pltpu.roll(stat, i, 0) for i in range(1, OWN)) + stat
    for c in range(PEERS):
        out_ref[pl.ds(c * CHUNK, OWN)] = out[c * OWN : (c + 1) * OWN]
        out_ref[pl.ds(c * CHUNK + OWN, 1)] = stat[(c + 1) * OWN - 1 : (c + 1) * OWN]


def merge_kernel(parts, out):
    stat = parts[pl.ds(OWN, PEERS, stride=CHUNK), :]
    high = jnp.max(stat, axis=0, keepdims=True)
    weight = jnp.exp2(jnp.minimum(stat - high, 0.0))
    total = jnp.sum(pltpu.roll(weight, OWN, 1) * stat, axis=0, keepdims=True)
    rows = []
    for r in range(OWN):
        part = parts[pl.ds(r, PEERS, stride=CHUNK), :]
        got = jnp.sum(part * weight[:, r : r + 1], axis=0, keepdims=True)
        rows.append(got / total[:, OWN + r : OWN + r + 1])
    out[...] = jnp.concatenate(rows, axis=0).astype(BF16)


def call(kernel, outs, specs, scratch=()):
    return pl.pallas_call(
        kernel,
        out_shape=outs,
        in_specs=specs,
        out_specs=VMEM,
        scratch_shapes=scratch,
        compiler_params=pltpu.CompilerParams(vmem_limit_bytes=VMEM_LIMIT),
    )


def turn(value, axis, step):
    size = lax.axis_size(axis)
    return lax.ppermute(value, axis, [(i, (i + step) % size) for i in range(size)])


def local(
    queries,
    row_branch,
    suffix_len,
    common_keys,
    common_values,
    branch_keys,
    branch_values,
    suffix_keys,
    suffix_values,
):
    ylo, z, x, yhi, core = (lax.axis_index(a) for a in ("ylo", "z", "x", "yhi", "core"))
    place = jnp.stack([ylo * N_Z + z, x, yhi, core]).astype(jnp.int32)
    width = KV_HEADS * HEAD_DIM
    flat = [
        a.reshape(-1, width)
        for a in (common_keys, common_values, branch_keys, branch_values, suffix_keys, suffix_values)
    ]
    packed = pl.pallas_call(
        pack_kernel,
        out_shape=[jax.ShapeDtypeStruct((2 * KEYS, HEAD_DIM), BF16)] * N_X,
        in_specs=[SMEM] + [ANY] * 6,
        out_specs=[ANY] * N_X,
        scratch_shapes=[pltpu.SemaphoreType.DMA((N_X, 6))],
    )(place, *flat)
    kvs = [packed[0]] + [turn(packed[i], "x", i) for i in range(1, N_X)]

    q = jnp.broadcast_to(queries[None], (PEERS, OWN, HEAD_DIM))
    q = lax.all_to_all(q, PLANE, split_axis=0, concat_axis=0, tiled=True)
    q = q.reshape(LINES, HEAD_DIM)
    parts = call(
        attend_kernel,
        jax.ShapeDtypeStruct((PEERS * CHUNK, HEAD_DIM), F32),
        [SMEM] * 3 + [VMEM] * 5,
        [pltpu.SMEM((8,), jnp.int32)],
    )(place, row_branch, suffix_len, q, *kvs)
    parts = parts.reshape(PEERS * CHUNK, 1, HEAD_DIM)
    parts = lax.all_to_all(parts, PLANE, split_axis=0, concat_axis=0, tiled=True)
    parts = parts.reshape(PEERS * CHUNK, HEAD_DIM)
    return call(merge_kernel, jax.ShapeDtypeStruct((OWN, HEAD_DIM), BF16), [VMEM])(parts)


def solution(mesh):
    axes = ("ylo", "z", "x", "yhi", "core")
    fine = Mesh(mesh.devices.reshape(N_YLO, N_Z, N_X, N_YHI, N_CORE), axes)
    branch, seq = ("ylo", "z"), ("x", "yhi", "core")
    return jax.shard_map(
        local,
        mesh=fine,
        in_specs=(
            P(branch, seq),
            P(),
            P(branch),
            P(branch + seq, None),
            P(branch + seq, None),
            P(branch, seq, None),
            P(branch, seq, None),
            P(branch, seq, None),
            P(branch, seq, None),
        ),
        out_specs=P(branch, seq),
        check_vma=False,
    )
```

time: 481 us -> 138 us (0.29)
  blocking collectives: 418 us -> 54.1 us
  Pallas kernels: 0 us -> 69.2 us
  waiting for transfers between devices: 28.5 us -> 0.01 us
  between operations: 15.1 us -> 0.1 us
  starting transfers between devices: 0.05 us -> 11.4 us
  local copies, waits for them, and re-layouts: 9.54 us -> 1.74 us
  matrix products: 5.72 us -> 0 us
    unnamed x2 -> x0, blocking collectives: 235 us -> none
    pmax x1 -> x0, blocking collectives: 101 us -> none  [local(): row_max = lax.pmax(local_max, ('branch', 'seq'))]
    all_gather x2 -> x0, blocking collectives: 81.2 us -> none  [the longest x1 47 us: local(): group_q = lax.all_gather(queries, 'seq', axis=1, tiled=True)]
    pallas_call x0 -> x3, Pallas kernels: none -> 69.2 us  [the longest x1 65.5 us: local(): pl.pallas_call(pack_kernel, out_shape=[jax.ShapeDtypeStruct((2 * KEYS, HE...]
    all_to_all x0 -> x2, blocking collectives: none -> 54.1 us  [the longest x1 31 us: local(): q = lax.all_to_all(q, PLANE, split_axis=0, concat_axis=0, tiled=True)]
    unnamed x4 -> x0, waiting for transfers between devices: 28.5 us -> none
    ppermute x0 -> x3, starting transfers between devices: none -> 11.4 us  [turn(): lax.ppermute(value, axis, [(i, (i + step) % size) for i in range(size)])]
    dot_general x10 -> x0, matrix products: 5.72 us -> none  [the longest x1 1.2 us: local(): jnp.einsum('rkgt,tkd->rkgd', branch_w.astype(jnp.bfloat16), val_branch, p...]
  transfers between devices with their start and end apart: 2 -> 3, of which waited for: 1 -> 0; matrix products, arithmetic and copies ran while one was open for 2% -> 0% of each run, Pallas kernels for 0% -> 0%
where the time goes in v1:
time: 138 us; the launch traced here: 137 us
  Pallas kernels  69.2 us (50%)
  blocking collectives  54.1 us (39%)
  starting transfers between devices  11.4 us (8%)
  local copies, waits for them, and re-layouts  1.74 us (1%)
    pallas_call x1, Pallas kernels, local(): pl.pallas_call(pack_kernel, out_shape=[jax.ShapeDtypeStruct((2 * KEYS, HE...  65.5 us
    all_to_all x1, blocking collectives, local(): q = lax.all_to_all(q, PLANE, split_axis=0, concat_axis=0, tiled=True)  31 us
    all_to_all x1, blocking collectives, local(): lax.all_to_all(parts, PLANE, split_axis=0, concat_axis=0, tiled=True)  23.1 us
    ppermute x3, starting transfers between devices, turn(): lax.ppermute(value, axis, [(i, (i + step) % size) for i in range(size)])  11.4 us
    pallas_call x1, Pallas kernels, local(): call(attend_kernel, jax.ShapeDtypeStruct((PEERS * CHUNK, HEAD_DIM), F32),...  2.95 us
  transfers between devices with their start and end apart: 3, of which 0 were waited for; matrix products, arithmetic and copies ran while one was open for 0% of the time, Pallas kernels for 0%

profile of v1, /device:TPU:1, one launch (start us, length us, event | category | flops | bytes accessed | tf_op | source)
XLA Modules:
  0.0 137.2 jit_solution(4288595120878705794)
XLA Ops:
  0.0 0.7 pad_add_fusion.place
  0.7 65.5 %shard_map.91 = (bf16[2048,128]{1,0:T(8,128)(2,1)}, bf16[2048,128]{1,0:T(8,128)(2,1)}, bf16[2048,128]{1,0:T(8,128)(2,1)}, bf16[2048,128]{1,0:T(8,128)(2,1)}) custom-call(s32[4]{0:T(128)} %pad_add_fusion.place, bf16[256,512]{1,0:T(8,128)(2,1)} %ck.1, bf16[256,512]{1,0:T(8,128)(2,1)} %cv.1, bf16[512,512]{1,0:T(8,128)(2,1)} %bitcast.16, ...), custom_call_target="tpu_custom_call" | custom-call | tf_op jit(solution)/shard_map/pallas_call | solution.py:192
  66.2 3.9 %collective-permute-start = (bf16[2048,128]{1,0:T(8,128)(2,1)}, bf16[2048,128]{1,0:T(8,128)(2,1)S(1)}, u32[]{:S(2)}, u32[]{:S(2)}) collective-permute-start(bf16[2048,128]{1,0:T(8,128)(2,1)} %get-tuple-element.10), channel_id=1, source_target_pairs={{0,8},{8,16},{16,24},{24,0},{1,9},{9,17},{17,25},{25,1},{2,10},{10... | collective-permute-start | bytes 1572872 | tf_op jit(solution)/shard_map/ppermute | solution.py:171
  70.1 0.0 copy-start.4
  70.1 4.4 %collective-permute-start.1 = (bf16[2048,128]{1,0:T(8,128)(2,1)}, bf16[2048,128]{1,0:T(8,128)(2,1)S(1)}, u32[]{:S(2)}, u32[]{:S(2)}) collective-permute-start(bf16[2048,128]{1,0:T(8,128)(2,1)} %get-tuple-element.11), channel_id=1, source_target_pairs={{0,16},{8,24},{16,0},{24,8},{1,17},{9,25},{17,1},{25,9},{2,18},{10... | collective-permute-start | bytes 1572872 | tf_op jit(solution)/shard_map/ppermute | solution.py:171
  74.5 3.1 %collective-permute-start.2 = (bf16[2048,128]{1,0:T(8,128)(2,1)}, bf16[2048,128]{1,0:T(8,128)(2,1)S(1)}, u32[]{:S(2)}, u32[]{:S(2)}) collective-permute-start(bf16[2048,128]{1,0:T(8,128)(2,1)} %get-tuple-element.12), channel_id=1, source_target_pairs={{0,24},{8,0},{16,8},{24,16},{1,25},{9,1},{17,9},{25,17},{2,26},{10... | collective-permute-start | bytes 1572872 | tf_op jit(solution)/shard_map/ppermute | solution.py:171
  77.6 0.0 copy-done.4
  77.6 31.0 %all_to_all.10 = bf16[128,4,128]{2,1,0:T(4,128)(2,1)S(1)} all-to-all(bf16[128,4,128]{2,1,0:T(4,128)(2,1)S(1)} %broadcast_in_dim.2), channel_id=1, replica_groups=mesh['ylo'=2,'z'=8,'x'=4,'yhi'=4,'core'=2] {'z','yhi','ylo','core'}, dimensions={0} | all-to-all | bytes 262144 | tf_op jit(solution)/shard_map/all_to_all | solution.py:202
  108.6 0.0 collective-permute-done.kv1
  108.6 0.0 collective-permute-done.1.kv2
  108.6 0.0 collective-permute-done.2.kv3
  108.6 0.0 copy-start.1
  108.6 0.0 copy-start.2
  108.6 0.0 copy-start.3
  108.6 0.6 copy-done.1
  109.3 0.0 copy-done.2
  109.3 0.0 copy-done.3
  109.3 0.0 copy-start
  109.3 1.0 copy-done
  110.3 3.0 %shard_map.92 = f32[640,128]{1,0:T(8,128)S(1)} custom-call(s32[4]{0:T(128)S(1)} %copy-done.1, s32[64]{0:T(128)S(1)} %copy-done.2, s32[4]{0:T(128)S(1)} %copy-done.3, bf16[512,128]{1,0:T(8,128)(2,1)S(1)} %bitcast.15, bf16[2048,128]{1,0:T(8,128)(2,1)S(1)} %copy-done, bf16[2048,128]{1,0:T(8,128)(2,1)S(1)} %collective-permute-done.kv1, ...), custom_call_target="tpu_custom_call" | custom-call | tf_op jit(solution)/shard_map/pallas_call | solution.py:204
  113.3 23.1 %all_to_all.11 = f32[640,1,128]{2,1,0:T(1,128)S(1)} all-to-all(f32[640,1,128]{2,1,0:T(1,128)S(1)} %bitcast.14), channel_id=1, replica_groups=mesh['ylo'=2,'z'=8,'x'=4,'yhi'=4,'core'=2] {'z','yhi','ylo','core'}, dimensions={0} | all-to-all | bytes 655360 | tf_op jit(solution)/shard_map/all_to_all | solution.py:211
  136.4 0.8 shard_map.93
  (1 shorter events, 0.0 us)
Async XLA Ops:
  66.2 42.4 %collective-permute-start = (bf16[2048,128]{1,0:T(8,128)(2,1)}, bf16[2048,128]{1,0:T(8,128)(2,1)S(1)}, u32[]{:S(2)}, u32[]{:S(2)}) collective-permute-start(bf16[2048,128]{1,0:T(8,128)(2,1)} %get-tuple-element.10), channel_id=1, source_target_pairs={{0,8},{8,16},{16,24},{24,0},{1,9},{9,17},{17,25},{25,1},{2,10},{10... | collective-permute-start | bytes 1572872 | tf_op jit(solution)/shard_map/ppermute | solution.py:171
  70.1 7.4 %copy-start.4 = (bf16[4,128]{1,0:T(4,128)(2,1)S(1)}, bf16[4,128]{1,0:T(4,128)(2,1)}, u32[]{:S(2)}) copy-start(bf16[4,128]{1,0:T(4,128)(2,1)} %param.9) | copy-start | bytes 3076
  70.1 38.5 %collective-permute-start.1 = (bf16[2048,128]{1,0:T(8,128)(2,1)}, bf16[2048,128]{1,0:T(8,128)(2,1)S(1)}, u32[]{:S(2)}, u32[]{:S(2)}) collective-permute-start(bf16[2048,128]{1,0:T(8,128)(2,1)} %get-tuple-element.11), channel_id=1, source_target_pairs={{0,16},{8,24},{16,0},{24,8},{1,17},{9,25},{17,1},{25,9},{2,18},{10... | collective-permute-start | bytes 1572872 | tf_op jit(solution)/shard_map/ppermute | solution.py:171
  74.5 34.1 %collective-permute-start.2 = (bf16[2048,128]{1,0:T(8,128)(2,1)}, bf16[2048,128]{1,0:T(8,128)(2,1)S(1)}, u32[]{:S(2)}, u32[]{:S(2)}) collective-permute-start(bf16[2048,128]{1,0:T(8,128)(2,1)} %get-tuple-element.12), channel_id=1, source_target_pairs={{0,24},{8,0},{16,8},{24,16},{1,25},{9,1},{17,9},{25,17},{2,26},{10... | collective-permute-start | bytes 1572872 | tf_op jit(solution)/shard_map/ppermute | solution.py:171
  108.6 0.7 copy-start.1
  108.6 0.7 copy-start.2
  108.6 0.7 copy-start.3
  109.3 1.0 copy-start

commit v2 on v1

--- a/solution.py
+++ b/solution.py
@@ -28,28 +28,46 @@
 BF16 = jnp.bfloat16
 SCALE = math.log2(math.e) / math.sqrt(HEAD_DIM)
 VMEM = pl.BlockSpec(memory_space=pltpu.VMEM)
-SMEM = pl.BlockSpec(memory_space=pltpu.SMEM)
 ANY = pl.BlockSpec(memory_space=pl.ANY)
 VMEM_LIMIT = 48 * 1024 * 1024
 
 
-def pack_kernel(place, ck, cv, bk, bv, sk, sv, *rest):
-    outs, sem = rest[:N_X], rest[N_X]
-    x = place[1]
-    copies = []
-    for i in range(N_X):
-        head = lax.rem(x + i, N_X)
-        cols = pl.ds(pl.multiple_of(head * HEAD_DIM, HEAD_DIM), HEAD_DIM)
-        at = 0
-        for n, (src, count) in enumerate(
-            ((ck, COM), (bk, BRA), (sk, OWN * SUF), (cv, COM), (bv, BRA), (sv, OWN * SUF))
-        ):
-            copy = pltpu.make_async_copy(src.at[:, cols], outs[i].at[pl.ds(at, count)], sem.at[i, n])
-            copy.start()
-            copies.append(copy)
-            at += count
-    for copy in copies:
+def pack_kernel(row_branch, suffix_len, ck, cv, bk, bv, sk, sv, *rest):
+    outs, info = rest[:N_X], rest[N_X]
+    held, branch_of, live, pick, sem = rest[N_X + 1 :]
+    x = lax.axis_index("x")
+    branch = lax.axis_index("ylo") * N_Z + lax.axis_index("z")
+    small = [
+        pltpu.make_async_copy(row_branch, branch_of, sem.at[6]),
+        pltpu.make_async_copy(suffix_len, live, sem.at[7]),
+    ]
+    copies, at = [], 0
+    for n, (src, count) in enumerate(
+        ((ck, COM), (bk, BRA), (sk, OWN * SUF), (cv, COM), (bv, BRA), (sv, OWN * SUF))
+    ):
+        rows = pl.ds(at, count)
+        copies.append((pltpu.make_async_copy(src, held.at[rows], sem.at[n]), rows))
+        at += count
+    for copy in small:
+        copy.start()
+    for copy, _ in copies:
+        copy.start()
+    for copy in small:
         copy.wait()
+    found = jnp.int32(0)
+    for i in range(ROWS):
+        pick[found] = jnp.int32(i)
+        found = found + (branch_of[i] == branch).astype(jnp.int32)
+    row = lax.broadcasted_iota(jnp.int32, info.shape, 0)
+    words = jnp.zeros(info.shape, jnp.int32)
+    for j in range(OWN):
+        words = jnp.where(row == j, pick[j], jnp.where(row == OWN + j, live[j], words))
+    info[...] = words
+    for copy, rows in copies:
+        copy.wait()
+        for i in range(N_X):
+            head = lax.rem(x + i, N_X)
+            outs[i][rows] = held[rows, pl.ds(pl.multiple_of(head * HEAD_DIM, HEAD_DIM), HEAD_DIM)]
 
 
 def attend(q, keys, values, mask=None):
@@ -69,17 +87,16 @@
     return out, top, jnp.sum(total, axis=1, keepdims=True)
 
 
-def attend_kernel(place, row_branch, suffix_len, q_ref, kv0, kv1, kv2, kv3, out_ref, pick):
-    branch, x, yhi, core = place[0], place[1], place[2], place[3]
+def attend_kernel(info, q_ref, kv0, kv1, kv2, kv3, out_ref):
+    x, yhi, core = (lax.axis_index(a) for a in ("x", "yhi", "core"))
+    branch = lax.axis_index("ylo") * N_Z + lax.axis_index("z")
     kvs = (kv0, kv1, kv2, kv3)
 
     def blocks(at, count):
         return [kv[pl.ds(at, count)] for kv in kvs], [kv[pl.ds(KEYS + at, count)] for kv in kvs]
 
-    found = jnp.int32(0)
-    for i in range(ROWS):
-        pick[found] = jnp.int32(i)
-        found = found + (row_branch[i] == branch).astype(jnp.int32)
+    def word(j, shape):
+        return jnp.broadcast_to(info[j : j + 1, 0:1], shape)
 
     q = q_ref[...]
     out, top, total = attend(q, *blocks(0, COM))
@@ -89,7 +106,7 @@
         slot = (at >> 3) & (OWN - 1)
         row = jnp.zeros(shape, jnp.int32)
         for j in range(OWN):
-            row = jnp.where(slot == j, jnp.where(at < PICKED, pick[j], branch * OWN + j), row)
+            row = jnp.where(slot == j, jnp.where(at < PICKED, word(j, shape), branch * OWN + j), row)
         ylo, z, r = row >> 5, (row >> 2) & 7, row & 3
         yh, co = (at >> 1) & 3, at & 1
         return (((z * N_YHI + yh) * N_YLO + ylo) * N_CORE + co) * OWN + r
@@ -105,7 +122,7 @@
     k_row, slot = slot >> 6, slot & (SUF - 1)
     live = jnp.zeros(shape, jnp.int32)
     for j in range(OWN):
-        live = jnp.where(k_row == j, suffix_len[j], live)
+        live = jnp.where(k_row == j, word(OWN + j, shape), live)
     mask = []
     for i in range(N_X):
         from_x = lax.rem(x + N_X - i, N_X)
@@ -160,7 +177,7 @@
         kernel,
         out_shape=outs,
         in_specs=specs,
-        out_specs=VMEM,
+        out_specs=jax.tree.map(lambda _: VMEM, outs),
         scratch_shapes=scratch,
         compiler_params=pltpu.CompilerParams(vmem_limit_bytes=VMEM_LIMIT),
     )
@@ -182,20 +199,24 @@
     suffix_keys,
     suffix_values,
 ):
-    ylo, z, x, yhi, core = (lax.axis_index(a) for a in ("ylo", "z", "x", "yhi", "core"))
-    place = jnp.stack([ylo * N_Z + z, x, yhi, core]).astype(jnp.int32)
     width = KV_HEADS * HEAD_DIM
     flat = [
         a.reshape(-1, width)
         for a in (common_keys, common_values, branch_keys, branch_values, suffix_keys, suffix_values)
     ]
-    packed = pl.pallas_call(
+    *packed, info = call(
         pack_kernel,
-        out_shape=[jax.ShapeDtypeStruct((2 * KEYS, HEAD_DIM), BF16)] * N_X,
-        in_specs=[SMEM] + [ANY] * 6,
-        out_specs=[ANY] * N_X,
-        scratch_shapes=[pltpu.SemaphoreType.DMA((N_X, 6))],
-    )(place, *flat)
+        [jax.ShapeDtypeStruct((2 * KEYS, HEAD_DIM), BF16)] * N_X
+        + [jax.ShapeDtypeStruct((2 * OWN, HEAD_DIM), jnp.int32)],
+        [ANY] * 8,
+        [
+            pltpu.VMEM((2 * KEYS, width), BF16),
+            pltpu.SMEM((ROWS,), jnp.int32),
+            pltpu.SMEM((OWN,), jnp.int32),
+            pltpu.SMEM((2 * OWN,), jnp.int32),
+            pltpu.SemaphoreType.DMA((8,)),
+        ],
+    )(row_branch, suffix_len, *flat)
     kvs = [packed[0]] + [turn(packed[i], "x", i) for i in range(1, N_X)]
 
     q = jnp.broadcast_to(queries[None], (PEERS, OWN, HEAD_DIM))
@@ -204,9 +225,8 @@
     parts = call(
         attend_kernel,
         jax.ShapeDtypeStruct((PEERS * CHUNK, HEAD_DIM), F32),
-        [SMEM] * 3 + [VMEM] * 5,
-        [pltpu.SMEM((8,), jnp.int32)],
-    )(place, row_branch, suffix_len, q, *kvs)
+        [VMEM] * 6,
+    )(info, q, *kvs)
     parts = parts.reshape(PEERS * CHUNK, 1, HEAD_DIM)
     parts = lax.all_to_all(parts, PLANE, split_axis=0, concat_axis=0, tiled=True)
     parts = parts.reshape(PEERS * CHUNK, HEAD_DIM)

time: 138 us -> 76.8 us (0.56)
  Pallas kernels: 69.2 us -> 4.31 us
  local copies, waits for them, and re-layouts: 1.74 us -> 6.59 us
    pallas_call x1, Pallas kernels: 65.5 us -> 1.14 us  [local(): call(pack_kernel, [jax.ShapeDtypeStruct((2 * KEYS, HEAD_DIM), BF16)] * N_...]
    unnamed x10 -> x18, local copies, waits for them, and re-layouts: 1.71 us -> 6.56 us
where the time goes in v2:
time: 76.8 us; the launch traced here: 76.2 us
  blocking collectives  53.9 us (70%)
  starting transfers between devices  11.4 us (15%)
  local copies, waits for them, and re-layouts  6.59 us (9%)
  Pallas kernels  4.31 us (6%)
    all_to_all x1, blocking collectives, local(): q = lax.all_to_all(q, PLANE, split_axis=0, concat_axis=0, tiled=True)  31 us
    all_to_all x1, blocking collectives, local(): lax.all_to_all(parts, PLANE, split_axis=0, concat_axis=0, tiled=True)  22.9 us
    ppermute x3, starting transfers between devices, turn(): lax.ppermute(value, axis, [(i, (i + step) % size) for i in range(size)])  11.4 us
    unnamed x18, local copies, waits for them, and re-layouts  6.56 us
    pallas_call x1, Pallas kernels, local(): call(attend_kernel, jax.ShapeDtypeStruct((PEERS * CHUNK, HEAD_DIM), F32),...  2.41 us
  transfers between devices with their start and end apart: 3, of which 0 were waited for; matrix products, arithmetic and copies ran while one was open for 0% of the time, Pallas kernels for 0%

profile of v2, /device:TPU:1, one launch (start us, length us, event | category | flops | bytes accessed | tf_op | source)
XLA Modules:
  0.0 76.2 jit_solution(16754029093470523253)
XLA Ops:
  0.0 0.0 copy-start.6
  0.0 0.0 copy-start.7
  0.0 0.7 copy-done.6
  0.7 0.0 copy-done.7
  0.7 0.0 copy-start
  0.7 1.0 %copy-done = bf16[1,512,512]{2,1,0:T(8,128)(2,1)S(1)} copy-done((bf16[1,512,512]{2,1,0:T(8,128)(2,1)S(1)}, bf16[1,512,512]{2,1,0:T(8,128)(2,1)}, u32[]{:S(2)}) %copy-start) | copy-done | bytes 524312
  1.7 0.0 copy-start.1
  1.7 1.0 %copy-done.1 = bf16[1,512,512]{2,1,0:T(8,128)(2,1)S(1)} copy-done((bf16[1,512,512]{2,1,0:T(8,128)(2,1)S(1)}, bf16[1,512,512]{2,1,0:T(8,128)(2,1)}, u32[]{:S(2)}) %copy-start.1) | copy-done | bytes 524312
  2.8 0.0 copy-start.2
  2.8 0.9 %copy-done.2 = bf16[256,512]{1,0:T(8,128)(2,1)S(1)} copy-done((bf16[256,512]{1,0:T(8,128)(2,1)S(1)}, bf16[256,512]{1,0:T(8,128)(2,1)}, u32[]{:S(2)}) %copy-start.2) | copy-done | bytes 262168
  3.7 0.0 copy-start.3
  3.7 0.9 %copy-done.3 = bf16[256,512]{1,0:T(8,128)(2,1)S(1)} copy-done((bf16[256,512]{1,0:T(8,128)(2,1)S(1)}, bf16[256,512]{1,0:T(8,128)(2,1)}, u32[]{:S(2)}) %copy-start.3) | copy-done | bytes 262168
  4.7 0.0 copy-start.4
  4.7 0.9 %copy-done.4 = bf16[4,64,512]{2,1,0:T(8,128)(2,1)S(1)} copy-done((bf16[4,64,512]{2,1,0:T(8,128)(2,1)S(1)}, bf16[4,64,512]{2,1,0:T(8,128)(2,1)}, u32[]{:S(2)}) %copy-start.4) | copy-done | bytes 262168
  5.6 0.0 copy-start.5
  5.6 0.9 %copy-done.5 = bf16[4,64,512]{2,1,0:T(8,128)(2,1)S(1)} copy-done((bf16[4,64,512]{2,1,0:T(8,128)(2,1)S(1)}, bf16[4,64,512]{2,1,0:T(8,128)(2,1)}, u32[]{:S(2)}) %copy-start.5) | copy-done | bytes 262168
  6.6 1.1 %shard_map.91 = (bf16[2048,128]{1,0:T(8,128)(2,1)S(1)}, bf16[2048,128]{1,0:T(8,128)(2,1)S(1)}, bf16[2048,128]{1,0:T(8,128)(2,1)S(1)}, bf16[2048,128]{1,0:T(8,128)(2,1)S(1)}, s32[8,128]{1,0:T(8,128)S(1)}) custom-call(s32[64]{0:T(128)S(1)} %copy-done.6, s32[4]{0:T(128)S(1)} %copy-done.7, bf16[256,512]{1,0:T(8,128)(2,1)S(1)} %copy-done.2, ...), custom_call_target="tpu_custom_call" | custom-call | tf_op jit(solution)/shard_map/pallas_call | solution.py:207
  7.7 3.9 %collective-permute-start = (bf16[2048,128]{1,0:T(8,128)(2,1)S(1)}, bf16[2048,128]{1,0:T(8,128)(2,1)S(1)}, u32[]{:S(2)}, u32[]{:S(2)}) collective-permute-start(bf16[2048,128]{1,0:T(8,128)(2,1)S(1)} %get-tuple-element.12), channel_id=1, source_target_pairs={{0,8},{8,16},{16,24},{24,0},{1,9},{9,17},{17,25},{25,1},{2,10},{10... | collective-permute-start | bytes 1572872 | tf_op jit(solution)/shard_map/ppermute | solution.py:188
  11.7 0.0 copy-start.8
  11.7 4.4 %collective-permute-start.1 = (bf16[2048,128]{1,0:T(8,128)(2,1)S(1)}, bf16[2048,128]{1,0:T(8,128)(2,1)S(1)}, u32[]{:S(2)}, u32[]{:S(2)}) collective-permute-start(bf16[2048,128]{1,0:T(8,128)(2,1)S(1)} %get-tuple-element.13), channel_id=1, source_target_pairs={{0,16},{8,24},{16,0},{24,8},{1,17},{9,25},{17,1},{25,9},{2,18},{10... | collective-permute-start | bytes 1572872 | tf_op jit(solution)/shard_map/ppermute | solution.py:188
  16.0 3.1 %collective-permute-start.2 = (bf16[2048,128]{1,0:T(8,128)(2,1)S(1)}, bf16[2048,128]{1,0:T(8,128)(2,1)S(1)}, u32[]{:S(2)}, u32[]{:S(2)}) collective-permute-start(bf16[2048,128]{1,0:T(8,128)(2,1)S(1)} %get-tuple-element.14), channel_id=1, source_target_pairs={{0,24},{8,0},{16,8},{24,16},{1,25},{9,1},{17,9},{25,17},{2,26},{10... | collective-permute-start | bytes 1572872 | tf_op jit(solution)/shard_map/ppermute | solution.py:188
  19.1 0.0 copy-done.8
  19.2 31.0 %all_to_all.10 = bf16[128,4,128]{2,1,0:T(4,128)(2,1)S(1)} all-to-all(bf16[128,4,128]{2,1,0:T(4,128)(2,1)S(1)} %broadcast_in_dim.2), channel_id=1, replica_groups=mesh['ylo'=2,'z'=8,'x'=4,'yhi'=4,'core'=2] {'z','yhi','ylo','core'}, dimensions={0} | all-to-all | bytes 262144 | tf_op jit(solution)/shard_map/all_to_all | solution.py:223
  50.1 0.0 collective-permute-done.kv1
  50.1 0.0 collective-permute-done.1.kv2
  50.1 0.0 collective-permute-done.2.kv3
  50.1 2.4 %shard_map.92 = f32[640,128]{1,0:T(8,128)S(1)} custom-call(s32[8,128]{1,0:T(8,128)S(1)} %get-tuple-element.10.info, bf16[512,128]{1,0:T(8,128)(2,1)S(1)} %bitcast.11, bf16[2048,128]{1,0:T(8,128)(2,1)S(1)} %get-tuple-element.11.kv0, bf16[2048,128]{1,0:T(8,128)(2,1)S(1)} %collective-permute-done.kv1, bf16[2048,128]{1,0:T(8,128)(2,1)S(1)} %collective-permute-done.1.kv2, ...), custom_call_target="tpu_custom_call" | custom-call | tf_op jit(solution)/shard_map/pallas_call | solution.py:225
  52.6 22.9 %all_to_all.11 = f32[640,1,128]{2,1,0:T(1,128)S(1)} all-to-all(f32[640,1,128]{2,1,0:T(1,128)S(1)} %bitcast.9), channel_id=1, replica_groups=mesh['ylo'=2,'z'=8,'x'=4,'yhi'=4,'core'=2] {'z','yhi','ylo','core'}, dimensions={0} | all-to-all | bytes 655360 | tf_op jit(solution)/shard_map/all_to_all | solution.py:231
  75.5 0.8 %shard_map.93 = bf16[4,128]{1,0:T(4,128)(2,1)} custom-call(f32[640,128]{1,0:T(8,128)S(1)} %bitcast.10), custom_call_target="tpu_custom_call" | custom-call | tf_op jit(solution)/shard_map/pallas_call | solution.py:233
  (1 shorter events, 0.0 us)
Async XLA Ops:
  0.0 0.7 copy-start.6
  0.0 0.7 copy-start.7
  0.7 1.0 %copy-start = (bf16[1,512,512]{2,1,0:T(8,128)(2,1)S(1)}, bf16[1,512,512]{2,1,0:T(8,128)(2,1)}, u32[]{:S(2)}) copy-start(bf16[1,512,512]{2,1,0:T(8,128)(2,1)} %param.14) | copy-start | bytes 1572868
  1.7 1.0 %copy-start.1 = (bf16[1,512,512]{2,1,0:T(8,128)(2,1)S(1)}, bf16[1,512,512]{2,1,0:T(8,128)(2,1)}, u32[]{:S(2)}) copy-start(bf16[1,512,512]{2,1,0:T(8,128)(2,1)} %param.15) | copy-start | bytes 1572868
  2.8 0.9 %copy-start.2 = (bf16[256,512]{1,0:T(8,128)(2,1)S(1)}, bf16[256,512]{1,0:T(8,128)(2,1)}, u32[]{:S(2)}) copy-start(bf16[256,512]{1,0:T(8,128)(2,1)} %ck.1) | copy-start | bytes 786436
  3.7 0.9 %copy-start.3 = (bf16[256,512]{1,0:T(8,128)(2,1)S(1)}, bf16[256,512]{1,0:T(8,128)(2,1)}, u32[]{:S(2)}) copy-start(bf16[256,512]{1,0:T(8,128)(2,1)} %cv.1) | copy-start | bytes 786436
  4.7 0.9 %copy-start.4 = (bf16[4,64,512]{2,1,0:T(8,128)(2,1)S(1)}, bf16[4,64,512]{2,1,0:T(8,128)(2,1)}, u32[]{:S(2)}) copy-start(bf16[4,64,512]{2,1,0:T(8,128)(2,1)} %param.16) | copy-start | bytes 786436
  5.6 0.9 %copy-start.5 = (bf16[4,64,512]{2,1,0:T(8,128)(2,1)S(1)}, bf16[4,64,512]{2,1,0:T(8,128)(2,1)}, u32[]{:S(2)}) copy-start(bf16[4,64,512]{2,1,0:T(8,128)(2,1)} %param.17) | copy-start | bytes 786436
  7.7 42.4 %collective-permute-start = (bf16[2048,128]{1,0:T(8,128)(2,1)S(1)}, bf16[2048,128]{1,0:T(8,128)(2,1)S(1)}, u32[]{:S(2)}, u32[]{:S(2)}) collective-permute-start(bf16[2048,128]{1,0:T(8,128)(2,1)S(1)} %get-tuple-element.12), channel_id=1, source_target_pairs={{0,8},{8,16},{16,24},{24,0},{1,9},{9,17},{17,25},{25,1},{2,10},{10... | collective-permute-start | bytes 1572872 | tf_op jit(solution)/shard_map/ppermute | solution.py:188
  11.7 7.5 %copy-start.8 = (bf16[4,128]{1,0:T(4,128)(2,1)S(1)}, bf16[4,128]{1,0:T(4,128)(2,1)}, u32[]{:S(2)}) copy-start(bf16[4,128]{1,0:T(4,128)(2,1)} %param.9) | copy-start | bytes 3076
  11.7 38.5 %collective-permute-start.1 = (bf16[2048,128]{1,0:T(8,128)(2,1)S(1)}, bf16[2048,128]{1,0:T(8,128)(2,1)S(1)}, u32[]{:S(2)}, u32[]{:S(2)}) collective-permute-start(bf16[2048,128]{1,0:T(8,128)(2,1)S(1)} %get-tuple-element.13), channel_id=1, source_target_pairs={{0,16},{8,24},{16,0},{24,8},{1,17},{9,25},{17,1},{25,9},{2,18},{10... | collective-permute-start | bytes 1572872 | tf_op jit(solution)/shard_map/ppermute | solution.py:188
  16.0 34.1 %collective-permute-start.2 = (bf16[2048,128]{1,0:T(8,128)(2,1)S(1)}, bf16[2048,128]{1,0:T(8,128)(2,1)S(1)}, u32[]{:S(2)}, u32[]{:S(2)}) collective-permute-start(bf16[2048,128]{1,0:T(8,128)(2,1)S(1)} %get-tuple-element.14), channel_id=1, source_target_pairs={{0,24},{8,0},{16,8},{24,16},{1,25},{9,1},{17,9},{25,17},{2,26},{10... | collective-permute-start | bytes 1572872 | tf_op jit(solution)/shard_map/ppermute | solution.py:188

commit v3 on v2

--- a/solution.py
+++ b/solution.py
@@ -28,13 +28,14 @@
 BF16 = jnp.bfloat16
 SCALE = math.log2(math.e) / math.sqrt(HEAD_DIM)
 VMEM = pl.BlockSpec(memory_space=pltpu.VMEM)
-ANY = pl.BlockSpec(memory_space=pl.ANY)
+HBM = pl.BlockSpec(memory_space=pltpu.HBM)
 VMEM_LIMIT = 48 * 1024 * 1024
+PACK_LIMIT = 57 * 1024 * 1024
 
 
 def pack_kernel(row_branch, suffix_len, ck, cv, bk, bv, sk, sv, *rest):
     outs, info = rest[:N_X], rest[N_X]
-    held, branch_of, live, pick, sem = rest[N_X + 1 :]
+    held, blocks, branch_of, live, pick, sem, out_sem = rest[N_X + 1 :]
     x = lax.axis_index("x")
     branch = lax.axis_index("ylo") * N_Z + lax.axis_index("z")
     small = [
@@ -48,10 +49,20 @@
         rows = pl.ds(at, count)
         copies.append((pltpu.make_async_copy(src, held.at[rows], sem.at[n]), rows))
         at += count
+    for copy, _ in copies:
+        copy.start()
     for copy in small:
         copy.start()
-    for copy, _ in copies:
-        copy.start()
+    sent = []
+    for n, (copy, rows) in enumerate(copies):
+        copy.wait()
+        for i in (1, 3, 2, 0):
+            head = lax.rem(x + i, N_X)
+            cols = pl.ds(pl.multiple_of(head * HEAD_DIM, HEAD_DIM), HEAD_DIM)
+            blocks[i, rows] = held[rows, cols]
+            out = pltpu.make_async_copy(blocks.at[i, rows], outs[i].at[rows], out_sem.at[i, n])
+            out.start()
+            sent.append(out)
     for copy in small:
         copy.wait()
     found = jnp.int32(0)
@@ -63,19 +74,18 @@
     for j in range(OWN):
         words = jnp.where(row == j, pick[j], jnp.where(row == OWN + j, live[j], words))
     info[...] = words
-    for copy, rows in copies:
-        copy.wait()
-        for i in range(N_X):
-            head = lax.rem(x + i, N_X)
-            outs[i][rows] = held[rows, pl.ds(pl.multiple_of(head * HEAD_DIM, HEAD_DIM), HEAD_DIM)]
-
-
-def attend(q, keys, values, mask=None):
+    for out in sent:
+        out.wait()
+
+
+def attend(q, keys, values, mask=None, before=None):
     scores = []
     for i, key in enumerate(keys):
         s = lax.dot_general(q, key, (((1,), (1,)), ((), ())), preferred_element_type=F32) * SCALE
         scores.append(s if mask is None else jnp.where(mask[i], s, LOW))
     top = jnp.max(functools.reduce(jnp.maximum, scores), axis=1, keepdims=True)
+    if before is not None:
+        top = jnp.maximum(top, before[1])
     total = out = None
     for i, (s, value) in enumerate(zip(scores, values)):
         w = jnp.exp2(s - top)
@@ -84,51 +94,77 @@
         o = jnp.dot(w.astype(BF16), value, preferred_element_type=F32)
         total = w if total is None else total + w
         out = o if out is None else out + o
-    return out, top, jnp.sum(total, axis=1, keepdims=True)
-
-
-def attend_kernel(info, q_ref, kv0, kv1, kv2, kv3, out_ref):
+    total = jnp.sum(total, axis=1, keepdims=True)
+    if before is not None:
+        scale = jnp.exp2(before[1] - top)
+        out, total = out + before[0] * scale, total + before[2] * scale
+    return out, top, total
+
+
+def attend_blocks(info, q, q_sel, kvs, steps, before):
     x, yhi, core = (lax.axis_index(a) for a in ("x", "yhi", "core"))
-    branch = lax.axis_index("ylo") * N_Z + lax.axis_index("z")
-    kvs = (kv0, kv1, kv2, kv3)
 
     def blocks(at, count):
         return [kv[pl.ds(at, count)] for kv in kvs], [kv[pl.ds(KEYS + at, count)] for kv in kvs]
 
-    def word(j, shape):
-        return jnp.broadcast_to(info[j : j + 1, 0:1], shape)
-
-    q = q_ref[...]
-    out, top, total = attend(q, *blocks(0, COM))
-
-    def lines(shape, axis):
-        at = lax.broadcasted_iota(jnp.int32, shape, axis)
-        slot = (at >> 3) & (OWN - 1)
-        row = jnp.zeros(shape, jnp.int32)
-        for j in range(OWN):
-            row = jnp.where(slot == j, jnp.where(at < PICKED, word(j, shape), branch * OWN + j), row)
-        ylo, z, r = row >> 5, (row >> 2) & 7, row & 3
-        yh, co = (at >> 1) & 3, at & 1
-        return (((z * N_YHI + yh) * N_YLO + ylo) * N_CORE + co) * OWN + r
-
-    shape = (2 * PICKED, LINES)
-    select = lax.broadcasted_iota(jnp.int32, shape, 1) == lines(shape, 0)
-    q_sel = jnp.dot(select.astype(F32).astype(BF16), q, preferred_element_type=F32).astype(BF16)
-    b_out, b_top, b_total = attend(q_sel[:PICKED], *blocks(COM, BRA))
-
+    common = attend(q, *blocks(0, COM), before=before[0])
+    branch = attend(q_sel[:PICKED], *blocks(COM, BRA), before=before[1])
     shape = (PICKED, OWN * SUF)
     q_row = lax.broadcasted_iota(jnp.int32, shape, 0) >> 3
     slot = lax.broadcasted_iota(jnp.int32, shape, 1)
     k_row, slot = slot >> 6, slot & (SUF - 1)
     live = jnp.zeros(shape, jnp.int32)
     for j in range(OWN):
-        live = jnp.where(k_row == j, word(OWN + j, shape), live)
+        live = jnp.where(k_row == j, word(info, OWN + j, shape), live)
     mask = []
-    for i in range(N_X):
-        from_x = lax.rem(x + N_X - i, N_X)
-        first = ((from_x * N_YHI + yhi) * N_CORE + core) * SUF
+    for i in steps:
+        first = ((lax.rem(x + N_X - i, N_X) * N_YHI + yhi) * N_CORE + core) * SUF
         mask.append((q_row == k_row) & (slot + first < live))
-    s_out, s_top, s_total = attend(q_sel[PICKED:], *blocks(COM + BRA, OWN * SUF), mask)
+    suffix = attend(q_sel[PICKED:], *blocks(COM + BRA, OWN * SUF), mask=mask, before=before[2])
+    return common, branch, suffix
+
+
+def word(info, j, shape):
+    return jnp.broadcast_to(info[j : j + 1, 0:1], shape)
+
+
+def picked_lines(info, shape, axis):
+    branch = lax.axis_index("ylo") * N_Z + lax.axis_index("z")
+    at = lax.broadcasted_iota(jnp.int32, shape, axis)
+    slot = (at >> 3) & (OWN - 1)
+    row = jnp.zeros(shape, jnp.int32)
+    for j in range(OWN):
+        row = jnp.where(slot == j, jnp.where(at < PICKED, word(info, j, shape), branch * OWN + j), row)
+    ylo, z, r = row >> 5, (row >> 2) & 7, row & 3
+    yhi, core = (at >> 1) & 3, at & 1
+    return (((z * N_YHI + yhi) * N_YLO + ylo) * N_CORE + core) * OWN + r
+
+
+PART_LINES = ((0, LINES), (LINES, PICKED), (LINES + PICKED, PICKED))
+ALL_LINES = LINES + 2 * PICKED
+
+
+def own_kernel(info, q_ref, kv, out_ref, stat_ref, sel_ref):
+    q = q_ref[...]
+    shape = (2 * PICKED, LINES)
+    select = lax.broadcasted_iota(jnp.int32, shape, 1) == picked_lines(info, shape, 0)
+    q_sel = jnp.dot(select.astype(F32).astype(BF16), q, preferred_element_type=F32).astype(BF16)
+    sel_ref[...] = q_sel
+    parts = attend_blocks(info, q, q_sel, [kv], [0], [None] * 3)
+    for (at, count), (out, top, total) in zip(PART_LINES, parts):
+        lane = lax.broadcasted_iota(jnp.int32, (count, HEAD_DIM), 1)
+        out_ref[pl.ds(at, count)] = out
+        stat_ref[pl.ds(at, count)] = jnp.where(lane == 0, top, total)
+
+
+def attend_kernel(info, q_ref, sel_ref, own_out, own_stat, kv1, kv2, kv3, out_ref):
+    before = []
+    for at, count in PART_LINES:
+        stat = own_stat[pl.ds(at, count)]
+        before.append((own_out[pl.ds(at, count)], stat[:, 0:1], stat[:, 1:2]))
+    (out, top, total), (b_out, b_top, b_total), (s_out, s_top, s_total) = attend_blocks(
+        info, q_ref[...], sel_ref[...], [kv1, kv2, kv3], [1, 2, 3], before
+    )
 
     square = (2 * PICKED, 2 * PICKED)
     eye = lax.broadcasted_iota(jnp.int32, square, 0) == lax.broadcasted_iota(jnp.int32, square, 1)
@@ -138,7 +174,7 @@
         return jnp.sum(jnp.where(eye, col, 0.0), axis=0, keepdims=True)
 
     shape = (LINES, 2 * PICKED)
-    place_of = lax.broadcasted_iota(jnp.int32, shape, 0) == lines(shape, 1)
+    place_of = lax.broadcasted_iota(jnp.int32, shape, 0) == picked_lines(info, shape, 1)
     p_top = jnp.where(place_of, jnp.broadcast_to(across(b_top, s_top), shape), LOW)
     high = jnp.maximum(top, jnp.max(p_top, axis=1, keepdims=True))
     weight = jnp.where(place_of, jnp.exp2(p_top - high), 0.0)
@@ -172,14 +208,14 @@
     out[...] = jnp.concatenate(rows, axis=0).astype(BF16)
 
 
-def call(kernel, outs, specs, scratch=()):
+def call(kernel, outs, specs, scratch=(), out_specs=None, limit=VMEM_LIMIT):
     return pl.pallas_call(
         kernel,
         out_shape=outs,
         in_specs=specs,
-        out_specs=jax.tree.map(lambda _: VMEM, outs),
+        out_specs=out_specs or jax.tree.map(lambda _: VMEM, outs),
         scratch_shapes=scratch,
-        compiler_params=pltpu.CompilerParams(vmem_limit_bytes=VMEM_LIMIT),
+        compiler_params=pltpu.CompilerParams(vmem_limit_bytes=limit),
     )
 
 
@@ -208,25 +244,37 @@
         pack_kernel,
         [jax.ShapeDtypeStruct((2 * KEYS, HEAD_DIM), BF16)] * N_X
         + [jax.ShapeDtypeStruct((2 * OWN, HEAD_DIM), jnp.int32)],
-        [ANY] * 8,
+        [HBM] * 8,
         [
             pltpu.VMEM((2 * KEYS, width), BF16),
+            pltpu.VMEM((N_X, 2 * KEYS, HEAD_DIM), BF16),
             pltpu.SMEM((ROWS,), jnp.int32),
             pltpu.SMEM((OWN,), jnp.int32),
             pltpu.SMEM((2 * OWN,), jnp.int32),
             pltpu.SemaphoreType.DMA((8,)),
+            pltpu.SemaphoreType.DMA((N_X, 6)),
         ],
+        [HBM] * N_X + [VMEM],
+        PACK_LIMIT,
     )(row_branch, suffix_len, *flat)
-    kvs = [packed[0]] + [turn(packed[i], "x", i) for i in range(1, N_X)]
+    kvs = {i: turn(packed[i], "x", i) for i in (1, 3, 2)}
+    kvs = [kvs[i] for i in range(1, N_X)]
 
     q = jnp.broadcast_to(queries[None], (PEERS, OWN, HEAD_DIM))
     q = lax.all_to_all(q, PLANE, split_axis=0, concat_axis=0, tiled=True)
     q = q.reshape(LINES, HEAD_DIM)
+    own_out, own_stat, sel = call(
+        own_kernel,
+        [
+            jax.ShapeDtypeStruct((ALL_LINES, HEAD_DIM), F32),
+            jax.ShapeDtypeStruct((ALL_LINES, HEAD_DIM), F32),
+            jax.ShapeDtypeStruct((2 * PICKED, HEAD_DIM), BF16),
+        ],
+        [VMEM] * 3,
+    )(info, q, packed[0])
     parts = call(
-        attend_kernel,
-        jax.ShapeDtypeStruct((PEERS * CHUNK, HEAD_DIM), F32),
-        [VMEM] * 6,
-    )(info, q, *kvs)
+        attend_kernel, jax.ShapeDtypeStruct((PEERS * CHUNK, HEAD_DIM), F32), [VMEM] * 8
+    )(info, q, sel, own_out, own_stat, *kvs)
     parts = parts.reshape(PEERS * CHUNK, 1, HEAD_DIM)
     parts = lax.all_to_all(parts, PLANE, split_axis=0, concat_axis=0, tiled=True)
     parts = parts.reshape(PEERS * CHUNK, HEAD_DIM)

time: 76.8 us -> 73.8 us (0.961)
  local copies, waits for them, and re-layouts: 6.59 us -> 1.77 us
  Pallas kernels: 4.31 us -> 7.63 us
  blocking collectives: 53.9 us -> 52.6 us
    unnamed x18 -> x6, local copies, waits for them, and re-layouts: 6.56 us -> 1.73 us
    pallas_call x1, Pallas kernels: 1.14 us -> 3.25 us  [local(): call(pack_kernel, [jax.ShapeDtypeStruct((2 * KEYS, HEAD_DIM), BF16)] * N_...]
    all_to_all x1, blocking collectives: 22.9 us -> 21.6 us  [local(): lax.all_to_all(parts, PLANE, split_axis=0, concat_axis=0, tiled=True)]
    pallas_call x0 -> x1, Pallas kernels: none -> 1 us  [local(): call(own_kernel, [jax.ShapeDtypeStruct((ALL_LINES, HEAD_DIM), F32), jax.S...]
  transfers between devices with their start and end apart: 3 -> 3, of which waited for: 0 -> 0; matrix products, arithmetic and copies ran while one was open for 0% -> 0% of each run, Pallas kernels for 0% -> 1%
where the time goes in v3:
time: 73.8 us; the launch traced here: 73.4 us
  blocking collectives  52.6 us (71%)
  starting transfers between devices  11.4 us (15%)
  Pallas kernels  7.63 us (10%)
  local copies, waits for them, and re-layouts  1.77 us (2%)
    all_to_all x1, blocking collectives, local(): q = lax.all_to_all(q, PLANE, split_axis=0, concat_axis=0, tiled=True)  31 us
    all_to_all x1, blocking collectives, local(): lax.all_to_all(parts, PLANE, split_axis=0, concat_axis=0, tiled=True)  21.6 us
    ppermute x3, starting transfers between devices, turn(): lax.ppermute(value, axis, [(i, (i + step) % size) for i in range(size)])  11.4 us
    pallas_call x1, Pallas kernels, local(): call(pack_kernel, [jax.ShapeDtypeStruct((2 * KEYS, HEAD_DIM), BF16)] * N_...  3.25 us
    pallas_call x1, Pallas kernels, local(): call(attend_kernel, jax.ShapeDtypeStruct((PEERS * CHUNK, HEAD_DIM), F32),...  2.61 us
    unnamed x6, local copies, waits for them, and re-layouts  1.73 us
  transfers between devices with their start and end apart: 3, of which 0 were waited for; matrix products, arithmetic and copies ran while one was open for 0% of the time, Pallas kernels for 1%

profile of v3, /device:TPU:1, one launch (start us, length us, event | category | flops | bytes accessed | tf_op | source)
XLA Modules:
  0.0 73.4 jit_solution(1734492363454632106)
XLA Ops:
  0.0 3.3 %shard_map.91 = (bf16[2048,128]{1,0:T(8,128)(2,1)}, bf16[2048,128]{1,0:T(8,128)(2,1)}, bf16[2048,128]{1,0:T(8,128)(2,1)}, bf16[2048,128]{1,0:T(8,128)(2,1)}, s32[8,128]{1,0:T(8,128)}) custom-call(s32[64]{0:T(128)} %row_branch.1, s32[4]{0:T(128)} %suffix_len.1, bf16[256,512]{1,0:T(8,128)(2,1)} %ck.1, bf16[256,512]{1,0:T(8,128)(2,1)} %cv.1, ...), custom_call_target="tpu_custom_call" | custom-call | tf_op jit(solution)/shard_map/pallas_call | solution.py:243
  3.3 3.9 %collective-permute-start = (bf16[2048,128]{1,0:T(8,128)(2,1)}, bf16[2048,128]{1,0:T(8,128)(2,1)S(1)}, u32[]{:S(2)}, u32[]{:S(2)}) collective-permute-start(bf16[2048,128]{1,0:T(8,128)(2,1)} %get-tuple-element.18), channel_id=1, source_target_pairs={{0,8},{8,16},{16,24},{24,0},{1,9},{9,17},{17,25},{25,1},{2,10},{10... | collective-permute-start | bytes 1572872 | tf_op jit(solution)/shard_map/ppermute | solution.py:224
  7.2 0.0 copy-start.2
  7.2 4.4 %collective-permute-start.1 = (bf16[2048,128]{1,0:T(8,128)(2,1)}, bf16[2048,128]{1,0:T(8,128)(2,1)S(1)}, u32[]{:S(2)}, u32[]{:S(2)}) collective-permute-start(bf16[2048,128]{1,0:T(8,128)(2,1)} %get-tuple-element.19), channel_id=1, source_target_pairs={{0,16},{8,24},{16,0},{24,8},{1,17},{9,25},{17,1},{25,9},{2,18},{10... | collective-permute-start | bytes 1572872 | tf_op jit(solution)/shard_map/ppermute | solution.py:224
  11.6 3.1 %collective-permute-start.2 = (bf16[2048,128]{1,0:T(8,128)(2,1)}, bf16[2048,128]{1,0:T(8,128)(2,1)S(1)}, u32[]{:S(2)}, u32[]{:S(2)}) collective-permute-start(bf16[2048,128]{1,0:T(8,128)(2,1)} %get-tuple-element.20), channel_id=1, source_target_pairs={{0,24},{8,0},{16,8},{24,16},{1,25},{9,1},{17,9},{25,17},{2,26},{10... | collective-permute-start | bytes 1572872 | tf_op jit(solution)/shard_map/ppermute | solution.py:224
  14.7 0.0 copy-done.2
  14.7 31.0 %all_to_all.10 = bf16[128,4,128]{2,1,0:T(4,128)(2,1)S(1)} all-to-all(bf16[128,4,128]{2,1,0:T(4,128)(2,1)S(1)} %broadcast_in_dim.2), channel_id=1, replica_groups=mesh['ylo'=2,'z'=8,'x'=4,'yhi'=4,'core'=2] {'z','yhi','ylo','core'}, dimensions={0} | all-to-all | bytes 262144 | tf_op jit(solution)/shard_map/all_to_all | solution.py:264
  45.7 0.0 copy-start.1
  45.7 0.7 copy-done.1
  46.4 0.0 copy-start
  46.4 1.0 %copy-done = bf16[2048,128]{1,0:T(8,128)(2,1)S(1)} copy-done((bf16[2048,128]{1,0:T(8,128)(2,1)S(1)}, bf16[2048,128]{1,0:T(8,128)(2,1)}, u32[]{:S(2)}) %copy-start) | copy-done | bytes 524312
  47.4 1.0 %shard_map.92 = (f32[576,128]{1,0:T(8,128)S(1)}, f32[576,128]{1,0:T(8,128)S(1)}, bf16[64,128]{1,0:T(8,128)(2,1)S(1)}) custom-call(s32[8,128]{1,0:T(8,128)S(1)} %copy-done.1, bf16[512,128]{1,0:T(8,128)(2,1)S(1)} %bitcast.11, bf16[2048,128]{1,0:T(8,128)(2,1)S(1)} %copy-done), custom_call_target="tpu_custom_call" | custom-call | tf_op jit(solution)/shard_map/pallas_call | solution.py:266
  48.4 0.0 collective-permute-done.kv1
  48.4 0.0 collective-permute-done.1.kv2
  48.4 0.0 collective-permute-done.2.kv3
  48.4 2.6 %shard_map.93 = f32[640,128]{1,0:T(8,128)S(1)} custom-call(s32[8,128]{1,0:T(8,128)S(1)} %copy-done.1, bf16[512,128]{1,0:T(8,128)(2,1)S(1)} %bitcast.12, bf16[64,128]{1,0:T(8,128)(2,1)S(1)} %get-tuple-element.15.sel_ref, f32[576,128]{1,0:T(8,128)S(1)} %get-tuple-element.16.own_out, f32[576,128]{1,0:T(8,128)S(1)} %get-tuple-element.17.own_stat, ...), custom_call_target="tpu_custom_call" | custom-call | tf_op jit(solution)/shard_map/pallas_call | solution.py:275
  51.1 21.6 %all_to_all.11 = f32[640,1,128]{2,1,0:T(1,128)S(1)} all-to-all(f32[640,1,128]{2,1,0:T(1,128)S(1)} %bitcast.9), channel_id=1, replica_groups=mesh['ylo'=2,'z'=8,'x'=4,'yhi'=4,'core'=2] {'z','yhi','ylo','core'}, dimensions={0} | all-to-all | bytes 655360 | tf_op jit(solution)/shard_map/all_to_all | solution.py:279
  72.7 0.8 %shard_map.94 = bf16[4,128]{1,0:T(4,128)(2,1)} custom-call(f32[640,128]{1,0:T(8,128)S(1)} %bitcast.10), custom_call_target="tpu_custom_call" | custom-call | tf_op jit(solution)/shard_map/pallas_call | solution.py:281
  (1 shorter events, 0.0 us)
Async XLA Ops:
  3.3 45.1 %collective-permute-start = (bf16[2048,128]{1,0:T(8,128)(2,1)}, bf16[2048,128]{1,0:T(8,128)(2,1)S(1)}, u32[]{:S(2)}, u32[]{:S(2)}) collective-permute-start(bf16[2048,128]{1,0:T(8,128)(2,1)} %get-tuple-element.18), channel_id=1, source_target_pairs={{0,8},{8,16},{16,24},{24,0},{1,9},{9,17},{17,25},{25,1},{2,10},{10... | collective-permute-start | bytes 1572872 | tf_op jit(solution)/shard_map/ppermute | solution.py:224
  7.2 7.4 %copy-start.2 = (bf16[4,128]{1,0:T(4,128)(2,1)S(1)}, bf16[4,128]{1,0:T(4,128)(2,1)}, u32[]{:S(2)}) copy-start(bf16[4,128]{1,0:T(4,128)(2,1)} %param.9) | copy-start | bytes 3076
  7.2 41.2 %collective-permute-start.1 = (bf16[2048,128]{1,0:T(8,128)(2,1)}, bf16[2048,128]{1,0:T(8,128)(2,1)S(1)}, u32[]{:S(2)}, u32[]{:S(2)}) collective-permute-start(bf16[2048,128]{1,0:T(8,128)(2,1)} %get-tuple-element.19), channel_id=1, source_target_pairs={{0,16},{8,24},{16,0},{24,8},{1,17},{9,25},{17,1},{25,9},{2,18},{10... | collective-permute-start | bytes 1572872 | tf_op jit(solution)/shard_map/ppermute | solution.py:224
  11.6 36.8 %collective-permute-start.2 = (bf16[2048,128]{1,0:T(8,128)(2,1)}, bf16[2048,128]{1,0:T(8,128)(2,1)S(1)}, u32[]{:S(2)}, u32[]{:S(2)}) collective-permute-start(bf16[2048,128]{1,0:T(8,128)(2,1)} %get-tuple-element.20), channel_id=1, source_target_pairs={{0,24},{8,0},{16,8},{24,16},{1,25},{9,1},{17,9},{25,17},{2,26},{10... | collective-permute-start | bytes 1572872 | tf_op jit(solution)/shard_map/ppermute | solution.py:224
  45.7 0.7 copy-start.1
  46.4 1.0 %copy-start = (bf16[2048,128]{1,0:T(8,128)(2,1)S(1)}, bf16[2048,128]{1,0:T(8,128)(2,1)}, u32[]{:S(2)}) copy-start(bf16[2048,128]{1,0:T(8,128)(2,1)} %get-tuple-element.14.kv) | copy-start | bytes 1572868

commit v4 on v2

--- a/solution.py
+++ b/solution.py
@@ -22,19 +22,22 @@
 KEYS = COM + BRA + OWN * SUF
 LINES = PEERS * OWN
 PICKED = OWN * GROUP
+INFO = 16
+OWN_ROOM = 1 << 16
 CHUNK = OWN + 1
 LOW = -1e30
 F32 = jnp.float32
 BF16 = jnp.bfloat16
 SCALE = math.log2(math.e) / math.sqrt(HEAD_DIM)
 VMEM = pl.BlockSpec(memory_space=pltpu.VMEM)
-ANY = pl.BlockSpec(memory_space=pl.ANY)
+HBM = pl.BlockSpec(memory_space=pltpu.HBM)
 VMEM_LIMIT = 48 * 1024 * 1024
+PACK_LIMIT = 57 * 1024 * 1024
 
 
 def pack_kernel(row_branch, suffix_len, ck, cv, bk, bv, sk, sv, *rest):
-    outs, info = rest[:N_X], rest[N_X]
-    held, branch_of, live, pick, sem = rest[N_X + 1 :]
+    outs = rest[:N_X]
+    held, blocks, info, branch_of, live, pick, sem, out_sem = rest[N_X:]
     x = lax.axis_index("x")
     branch = lax.axis_index("ylo") * N_Z + lax.axis_index("z")
     small = [
@@ -48,9 +51,7 @@
         rows = pl.ds(at, count)
         copies.append((pltpu.make_async_copy(src, held.at[rows], sem.at[n]), rows))
         at += count
-    for copy in small:
-        copy.start()
-    for copy, _ in copies:
+    for copy in (*small, *(copy for copy, _ in copies)):
         copy.start()
     for copy in small:
         copy.wait()
@@ -61,60 +62,83 @@
     row = lax.broadcasted_iota(jnp.int32, info.shape, 0)
     words = jnp.zeros(info.shape, jnp.int32)
     for j in range(OWN):
-        words = jnp.where(row == j, pick[j], jnp.where(row == OWN + j, live[j], words))
-    info[...] = words
-    for copy, rows in copies:
+        words = jnp.where(row == j, pick[j], words)
+        words = jnp.where(row == OWN + j, live[j] >> 4, words)
+        words = jnp.where(row == 2 * OWN + j, live[j] & 15, words)
+    info[...] = words.astype(F32).astype(BF16)
+    sent = [pltpu.make_async_copy(info, outs[0].at[pl.ds(2 * KEYS, INFO)], out_sem.at[0, 6])]
+    sent[0].start()
+    for n, (copy, rows) in enumerate(copies):
         copy.wait()
-        for i in range(N_X):
+        for i in (1, 3, 2, 0):
             head = lax.rem(x + i, N_X)
-            outs[i][rows] = held[rows, pl.ds(pl.multiple_of(head * HEAD_DIM, HEAD_DIM), HEAD_DIM)]
-
-
-def attend(q, keys, values, mask=None):
-    scores = []
-    for i, key in enumerate(keys):
-        s = lax.dot_general(q, key, (((1,), (1,)), ((), ())), preferred_element_type=F32) * SCALE
-        scores.append(s if mask is None else jnp.where(mask[i], s, LOW))
+            cols = pl.ds(pl.multiple_of(head * HEAD_DIM, HEAD_DIM), HEAD_DIM)
+            blocks[i, rows] = held[rows, cols]
+            out = pltpu.make_async_copy(blocks.at[i, rows], outs[i].at[rows], out_sem.at[i, n])
+            out.start()
+            sent.append(out)
+    for out in sent:
+        out.wait()
+
+
+def score(q, key, mask=None):
+    s = lax.dot_general(q, key, (((1,), (1,)), ((), ())), preferred_element_type=F32) * SCALE
+    return s if mask is None else jnp.where(mask, s, LOW)
+
+
+def weigh(scores, values, masks=None):
     top = jnp.max(functools.reduce(jnp.maximum, scores), axis=1, keepdims=True)
     total = out = None
     for i, (s, value) in enumerate(zip(scores, values)):
         w = jnp.exp2(s - top)
-        if mask is not None:
-            w = jnp.where(mask[i], w, 0.0)
+        if masks is not None:
+            w = jnp.where(masks[i], w, 0.0)
         o = jnp.dot(w.astype(BF16), value, preferred_element_type=F32)
         total = w if total is None else total + w
         out = o if out is None else out + o
     return out, top, jnp.sum(total, axis=1, keepdims=True)
 
 
-def attend_kernel(info, q_ref, kv0, kv1, kv2, kv3, out_ref):
+def picked_lines(picks, shape, axis):
+    branch = lax.axis_index("ylo") * N_Z + lax.axis_index("z")
+    at = lax.broadcasted_iota(jnp.int32, shape, axis)
+    slot = (at >> 3) & (OWN - 1)
+    row = branch * OWN + slot
+    for j in range(OWN):
+        row = jnp.where(at >> 3 == j, jnp.broadcast_to(picks[j], shape), row)
+    ylo, z, r = row >> 5, (row >> 2) & 7, row & 3
+    yhi, core = (at >> 1) & 3, at & 1
+    return (((z * N_YHI + yhi) * N_YLO + ylo) * N_CORE + core) * OWN + r
+
+
+def attend_kernel(own_hbm, q_ref, kv1, kv2, kv3, out_ref, own, sem):
     x, yhi, core = (lax.axis_index(a) for a in ("x", "yhi", "core"))
-    branch = lax.axis_index("ylo") * N_Z + lax.axis_index("z")
-    kvs = (kv0, kv1, kv2, kv3)
-
-    def blocks(at, count):
-        return [kv[pl.ds(at, count)] for kv in kvs], [kv[pl.ds(KEYS + at, count)] for kv in kvs]
-
-    def word(j, shape):
-        return jnp.broadcast_to(info[j : j + 1, 0:1], shape)
+    load = pltpu.make_async_copy(own_hbm.at[pl.ds(0, 2 * KEYS + INFO)], own, sem)
+    load.start()
+    kvs = [kv1, kv2, kv3, own]
+    sources = [lax.rem(x + N_X - i, N_X) for i in (1, 2, 3, 0)]
+
+    def key(kv, at, count):
+        return kv[pl.ds(at, count)]
+
+    def values(at, count):
+        return [kv[pl.ds(KEYS + at, count)] for kv in kvs]
 
     q = q_ref[...]
-    out, top, total = attend(q, *blocks(0, COM))
-
-    def lines(shape, axis):
-        at = lax.broadcasted_iota(jnp.int32, shape, axis)
-        slot = (at >> 3) & (OWN - 1)
-        row = jnp.zeros(shape, jnp.int32)
-        for j in range(OWN):
-            row = jnp.where(slot == j, jnp.where(at < PICKED, word(j, shape), branch * OWN + j), row)
-        ylo, z, r = row >> 5, (row >> 2) & 7, row & 3
-        yh, co = (at >> 1) & 3, at & 1
-        return (((z * N_YHI + yh) * N_YLO + ylo) * N_CORE + co) * OWN + r
-
+    scores = [score(q, key(kv, 0, COM)) for kv in kvs[:-1]]
+    load.wait()
+    scores.append(score(q, key(own, 0, COM)))
+    out, top, total = weigh(scores, values(0, COM))
+
+    info = own[pl.ds(2 * KEYS, INFO)].astype(F32).astype(jnp.int32)
+    words = [info[j : j + 1, 0:1] for j in range(3 * OWN)]
+    picks = words[:OWN]
+    lives = [16 * words[OWN + j] + words[2 * OWN + j] for j in range(OWN)]
     shape = (2 * PICKED, LINES)
-    select = lax.broadcasted_iota(jnp.int32, shape, 1) == lines(shape, 0)
+    select = lax.broadcasted_iota(jnp.int32, shape, 1) == picked_lines(picks, shape, 0)
     q_sel = jnp.dot(select.astype(F32).astype(BF16), q, preferred_element_type=F32).astype(BF16)
-    b_out, b_top, b_total = attend(q_sel[:PICKED], *blocks(COM, BRA))
+    scores = [score(q_sel[:PICKED], key(kv, COM, BRA)) for kv in kvs]
+    b_out, b_top, b_total = weigh(scores, values(COM, BRA))
 
     shape = (PICKED, OWN * SUF)
     q_row = lax.broadcasted_iota(jnp.int32, shape, 0) >> 3
@@ -122,13 +146,14 @@
     k_row, slot = slot >> 6, slot & (SUF - 1)
     live = jnp.zeros(shape, jnp.int32)
     for j in range(OWN):
-        live = jnp.where(k_row == j, word(OWN + j, shape), live)
-    mask = []
-    for i in range(N_X):
-        from_x = lax.rem(x + N_X - i, N_X)
-        first = ((from_x * N_YHI + yhi) * N_CORE + core) * SUF
-        mask.append((q_row == k_row) & (slot + first < live))
-    s_out, s_top, s_total = attend(q_sel[PICKED:], *blocks(COM + BRA, OWN * SUF), mask)
+        live = jnp.where(k_row == j, jnp.broadcast_to(lives[j], shape), live)
+    masks = []
+    for source in sources:
+        first = ((source * N_YHI + yhi) * N_CORE + core) * SUF
+        masks.append((q_row == k_row) & (slot + first < live))
+    suffix = (COM + BRA, OWN * SUF)
+    scores = [score(q_sel[PICKED:], key(kv, *suffix), mask) for kv, mask in zip(kvs, masks)]
+    s_out, s_top, s_total = weigh(scores, values(*suffix), masks)
 
     square = (2 * PICKED, 2 * PICKED)
     eye = lax.broadcasted_iota(jnp.int32, square, 0) == lax.broadcasted_iota(jnp.int32, square, 1)
@@ -138,7 +163,7 @@
         return jnp.sum(jnp.where(eye, col, 0.0), axis=0, keepdims=True)
 
     shape = (LINES, 2 * PICKED)
-    place_of = lax.broadcasted_iota(jnp.int32, shape, 0) == lines(shape, 1)
+    place_of = lax.broadcasted_iota(jnp.int32, shape, 0) == picked_lines(picks, shape, 1)
     p_top = jnp.where(place_of, jnp.broadcast_to(across(b_top, s_top), shape), LOW)
     high = jnp.maximum(top, jnp.max(p_top, axis=1, keepdims=True))
     weight = jnp.where(place_of, jnp.exp2(p_top - high), 0.0)
@@ -172,14 +197,14 @@
     out[...] = jnp.concatenate(rows, axis=0).astype(BF16)
 
 
-def call(kernel, outs, specs, scratch=()):
+def call(kernel, outs, specs, scratch=(), out_specs=None, limit=VMEM_LIMIT):
     return pl.pallas_call(
         kernel,
         out_shape=outs,
         in_specs=specs,
-        out_specs=jax.tree.map(lambda _: VMEM, outs),
+        out_specs=out_specs or jax.tree.map(lambda _: VMEM, outs),
         scratch_shapes=scratch,
-        compiler_params=pltpu.CompilerParams(vmem_limit_bytes=VMEM_LIMIT),
+        compiler_params=pltpu.CompilerParams(vmem_limit_bytes=limit),
     )
 
 
@@ -204,20 +229,28 @@
         a.reshape(-1, width)
         for a in (common_keys, common_values, branch_keys, branch_values, suffix_keys, suffix_values)
     ]
-    *packed, info = call(
+    block = (2 * KEYS, HEAD_DIM)
+    block = (2 * KEYS, HEAD_DIM)
+    packed = call(
         pack_kernel,
-        [jax.ShapeDtypeStruct((2 * KEYS, HEAD_DIM), BF16)] * N_X
-        + [jax.ShapeDtypeStruct((2 * OWN, HEAD_DIM), jnp.int32)],
-        [ANY] * 8,
+        [jax.ShapeDtypeStruct((OWN_ROOM, HEAD_DIM), BF16)]
+        + [jax.ShapeDtypeStruct(block, BF16)] * (N_X - 1),
+        [HBM] * 8,
         [
             pltpu.VMEM((2 * KEYS, width), BF16),
+            pltpu.VMEM((N_X, *block), BF16),
+            pltpu.VMEM((INFO, HEAD_DIM), BF16),
             pltpu.SMEM((ROWS,), jnp.int32),
             pltpu.SMEM((OWN,), jnp.int32),
             pltpu.SMEM((2 * OWN,), jnp.int32),
             pltpu.SemaphoreType.DMA((8,)),
+            pltpu.SemaphoreType.DMA((N_X, 7)),
         ],
+        [HBM] * N_X,
+        PACK_LIMIT,
     )(row_branch, suffix_len, *flat)
-    kvs = [packed[0]] + [turn(packed[i], "x", i) for i in range(1, N_X)]
+    kvs = {i: turn(packed[i], "x", i) for i in (1, 3, 2)}
+    kvs = [kvs[i] for i in range(1, N_X)]
 
     q = jnp.broadcast_to(queries[None], (PEERS, OWN, HEAD_DIM))
     q = lax.all_to_all(q, PLANE, split_axis=0, concat_axis=0, tiled=True)
@@ -225,8 +258,9 @@
     parts = call(
         attend_kernel,
         jax.ShapeDtypeStruct((PEERS * CHUNK, HEAD_DIM), F32),
-        [VMEM] * 6,
-    )(info, q, *kvs)
+        [HBM] + [VMEM] * 4,
+        [pltpu.VMEM((2 * KEYS + INFO, HEAD_DIM), BF16), pltpu.SemaphoreType.DMA],
+    )(packed[0], q, *kvs)
     parts = parts.reshape(PEERS * CHUNK, 1, HEAD_DIM)
     parts = lax.all_to_all(parts, PLANE, split_axis=0, concat_axis=0, tiled=True)
     parts = parts.reshape(PEERS * CHUNK, HEAD_DIM)

time: 76.8 us -> 72.6 us (0.945)
  local copies, waits for them, and re-layouts: 6.59 us -> 0.72 us
  Pallas kernels: 4.31 us -> 6.61 us
    unnamed x18 -> x0, local copies, waits for them, and re-layouts: 6.56 us -> none
    pallas_call x1, Pallas kernels: 1.14 us -> 2.73 us  [local(): call(pack_kernel, [jax.ShapeDtypeStruct((OWN_ROOM, HEAD_DIM), BF16)] + [j...]
  transfers between devices with their start and end apart: 3 -> 3, of which waited for: 0 -> 0; matrix products, arithmetic and copies ran while one was open for 0% -> 1% of each run, Pallas kernels for 0% -> 0%
where the time goes in v4:
time: 72.6 us; the launch traced here: 72.2 us
  blocking collectives  53.4 us (74%)
  starting transfers between devices  11.4 us (16%)
  Pallas kernels  6.61 us (9%)
    all_to_all x1, blocking collectives, local(): q = lax.all_to_all(q, PLANE, split_axis=0, concat_axis=0, tiled=True)  31 us
    all_to_all x1, blocking collectives, local(): lax.all_to_all(parts, PLANE, split_axis=0, concat_axis=0, tiled=True)  22.5 us
    ppermute x3, starting transfers between devices, turn(): lax.ppermute(value, axis, [(i, (i + step) % size) for i in range(size)])  11.4 us
    pallas_call x1, Pallas kernels, local(): call(attend_kernel, jax.ShapeDtypeStruct((PEERS * CHUNK, HEAD_DIM), F32),...  3.11 us
    pallas_call x1, Pallas kernels, local(): call(pack_kernel, [jax.ShapeDtypeStruct((OWN_ROOM, HEAD_DIM), BF16)] + [j...  2.73 us
  transfers between devices with their start and end apart: 3, of which 0 were waited for; matrix products, arithmetic and copies ran while one was open for 1% of the time, Pallas kernels for 0%

profile of v4, /device:TPU:1, one launch (start us, length us, event | category | flops | bytes accessed | tf_op | source)
XLA Modules:
  0.0 72.2 jit_solution(18312671607794492803)
XLA Ops:
  0.0 2.7 %shard_map.91 = (bf16[65536,128]{1,0:T(8,128)(2,1)}, bf16[2048,128]{1,0:T(8,128)(2,1)}, bf16[2048,128]{1,0:T(8,128)(2,1)}, bf16[2048,128]{1,0:T(8,128)(2,1)}) custom-call(s32[64]{0:T(128)} %row_branch.1, s32[4]{0:T(128)} %suffix_len.1, bf16[256,512]{1,0:T(8,128)(2,1)} %ck.1, bf16[256,512]{1,0:T(8,128)(2,1)} %cv.1, bf16[512,512]{1,0:T(8,128)(2,1)} %bitcast.12, ...), custom_call_target="tpu_custom_call" | custom-call | tf_op jit(solution)/shard_map/pallas_call | solution.py:234
  2.7 3.9 %collective-permute-start = (bf16[2048,128]{1,0:T(8,128)(2,1)}, bf16[2048,128]{1,0:T(8,128)(2,1)S(1)}, u32[]{:S(2)}, u32[]{:S(2)}) collective-permute-start(bf16[2048,128]{1,0:T(8,128)(2,1)} %get-tuple-element.10), channel_id=1, source_target_pairs={{0,8},{8,16},{16,24},{24,0},{1,9},{9,17},{17,25},{25,1},{2,10},{10... | collective-permute-start | bytes 1572872 | tf_op jit(solution)/shard_map/ppermute | solution.py:213
  6.7 4.4 %collective-permute-start.1 = (bf16[2048,128]{1,0:T(8,128)(2,1)}, bf16[2048,128]{1,0:T(8,128)(2,1)S(1)}, u32[]{:S(2)}, u32[]{:S(2)}) collective-permute-start(bf16[2048,128]{1,0:T(8,128)(2,1)} %get-tuple-element.11), channel_id=1, source_target_pairs={{0,16},{8,24},{16,0},{24,8},{1,17},{9,25},{17,1},{25,9},{2,18},{10... | collective-permute-start | bytes 1572872 | tf_op jit(solution)/shard_map/ppermute | solution.py:213
  11.1 3.1 %collective-permute-start.2 = (bf16[2048,128]{1,0:T(8,128)(2,1)}, bf16[2048,128]{1,0:T(8,128)(2,1)S(1)}, u32[]{:S(2)}, u32[]{:S(2)}) collective-permute-start(bf16[2048,128]{1,0:T(8,128)(2,1)} %get-tuple-element.12), channel_id=1, source_target_pairs={{0,24},{8,0},{16,8},{24,16},{1,25},{9,1},{17,9},{25,17},{2,26},{10... | collective-permute-start | bytes 1572872 | tf_op jit(solution)/shard_map/ppermute | solution.py:213
  14.1 0.7 broadcast_in_dim.2
  14.9 31.0 %all_to_all.10 = bf16[128,4,128]{2,1,0:T(4,128)(2,1)S(1)} all-to-all(bf16[128,4,128]{2,1,0:T(4,128)(2,1)S(1)} %broadcast_in_dim.2), channel_id=1, replica_groups=mesh['ylo'=2,'z'=8,'x'=4,'yhi'=4,'core'=2] {'z','yhi','ylo','core'}, dimensions={0} | all-to-all | bytes 262144 | tf_op jit(solution)/shard_map/all_to_all | solution.py:256
  45.8 0.0 collective-permute-done.kv1
  45.8 0.0 collective-permute-done.1.kv2
  45.8 0.0 collective-permute-done.2.kv3
  45.8 3.1 %shard_map.92 = f32[640,128]{1,0:T(8,128)S(1)} custom-call(bf16[65536,128]{1,0:T(8,128)(2,1)} %get-tuple-element.9.own_hbm, bf16[512,128]{1,0:T(8,128)(2,1)S(1)} %bitcast.11, bf16[2048,128]{1,0:T(8,128)(2,1)S(1)} %collective-permute-done.kv1, bf16[2048,128]{1,0:T(8,128)(2,1)S(1)} %collective-permute-done.1.kv2, bf16[2048,128]{1,0:T(8,128)(2,1)S(1)} %collective-permute-done.2.kv3), custom_call_target="tpu_custom_call" | custom-call | tf_op jit(solution)/shard_map/pallas_call | solution.py:258
  48.9 22.5 %all_to_all.11 = f32[640,1,128]{2,1,0:T(1,128)S(1)} all-to-all(f32[640,1,128]{2,1,0:T(1,128)S(1)} %bitcast.10), channel_id=1, replica_groups=mesh['ylo'=2,'z'=8,'x'=4,'yhi'=4,'core'=2] {'z','yhi','ylo','core'}, dimensions={0} | all-to-all | bytes 655360 | tf_op jit(solution)/shard_map/all_to_all | solution.py:265
  71.4 0.8 %shard_map.93 = bf16[4,128]{1,0:T(4,128)(2,1)} custom-call(f32[640,128]{1,0:T(8,128)S(1)} %bitcast.9), custom_call_target="tpu_custom_call" | custom-call | tf_op jit(solution)/shard_map/pallas_call | solution.py:267
Async XLA Ops:
  2.7 43.1 %collective-permute-start = (bf16[2048,128]{1,0:T(8,128)(2,1)}, bf16[2048,128]{1,0:T(8,128)(2,1)S(1)}, u32[]{:S(2)}, u32[]{:S(2)}) collective-permute-start(bf16[2048,128]{1,0:T(8,128)(2,1)} %get-tuple-element.10), channel_id=1, source_target_pairs={{0,8},{8,16},{16,24},{24,0},{1,9},{9,17},{17,25},{25,1},{2,10},{10... | collective-permute-start | bytes 1572872 | tf_op jit(solution)/shard_map/ppermute | solution.py:213
  6.7 39.1 %collective-permute-start.1 = (bf16[2048,128]{1,0:T(8,128)(2,1)}, bf16[2048,128]{1,0:T(8,128)(2,1)S(1)}, u32[]{:S(2)}, u32[]{:S(2)}) collective-permute-start(bf16[2048,128]{1,0:T(8,128)(2,1)} %get-tuple-element.11), channel_id=1, source_target_pairs={{0,16},{8,24},{16,0},{24,8},{1,17},{9,25},{17,1},{25,9},{2,18},{10... | collective-permute-start | bytes 1572872 | tf_op jit(solution)/shard_map/ppermute | solution.py:213
  11.1 34.8 %collective-permute-start.2 = (bf16[2048,128]{1,0:T(8,128)(2,1)}, bf16[2048,128]{1,0:T(8,128)(2,1)S(1)}, u32[]{:S(2)}, u32[]{:S(2)}) collective-permute-start(bf16[2048,128]{1,0:T(8,128)(2,1)} %get-tuple-element.12), channel_id=1, source_target_pairs={{0,24},{8,0},{16,8},{24,16},{1,25},{9,1},{17,9},{25,17},{2,26},{10... | collective-permute-start | bytes 1572872 | tf_op jit(solution)/shard_map/ppermute | solution.py:213

commit v5 on v4

--- a/solution.py
+++ b/solution.py
@@ -35,14 +35,15 @@
 PACK_LIMIT = 57 * 1024 * 1024
 
 
-def pack_kernel(row_branch, suffix_len, ck, cv, bk, bv, sk, sv, *rest):
-    outs = rest[:N_X]
-    held, blocks, info, branch_of, live, pick, sem, out_sem = rest[N_X:]
+def pack_kernel(queries, row_branch, suffix_len, ck, cv, bk, bv, sk, sv, *rest):
+    repeated, outs = rest[0], rest[1 : 1 + N_X]
+    held, blocks, info, lines, line_room, branch_of, live, pick, sem, out_sem = rest[1 + N_X :]
     x = lax.axis_index("x")
     branch = lax.axis_index("ylo") * N_Z + lax.axis_index("z")
     small = [
         pltpu.make_async_copy(row_branch, branch_of, sem.at[6]),
         pltpu.make_async_copy(suffix_len, live, sem.at[7]),
+        pltpu.make_async_copy(queries, lines, sem.at[8]),
     ]
     copies, at = [], 0
     for n, (src, count) in enumerate(
@@ -66,8 +67,13 @@
         words = jnp.where(row == OWN + j, live[j] >> 4, words)
         words = jnp.where(row == 2 * OWN + j, live[j] & 15, words)
     info[...] = words.astype(F32).astype(BF16)
-    sent = [pltpu.make_async_copy(info, outs[0].at[pl.ds(2 * KEYS, INFO)], out_sem.at[0, 6])]
-    sent[0].start()
+    line_room[...] = jnp.broadcast_to(lines[...], line_room.shape)
+    sent = [
+        pltpu.make_async_copy(info, outs[0].at[pl.ds(2 * KEYS, INFO)], out_sem.at[0, 6]),
+        pltpu.make_async_copy(line_room, repeated, out_sem.at[1, 6]),
+    ]
+    for out in sent:
+        out.start()
     for n, (copy, rows) in enumerate(copies):
         copy.wait()
         for i in (1, 3, 2, 0):
@@ -99,11 +105,11 @@
     return out, top, jnp.sum(total, axis=1, keepdims=True)
 
 
-def picked_lines(picks, shape, axis):
+def picked_lines(picks, axis):
+    shape = (2 * PICKED, 1) if axis == 0 else (1, 2 * PICKED)
     branch = lax.axis_index("ylo") * N_Z + lax.axis_index("z")
     at = lax.broadcasted_iota(jnp.int32, shape, axis)
-    slot = (at >> 3) & (OWN - 1)
-    row = branch * OWN + slot
+    row = branch * OWN + ((at >> 3) & (OWN - 1))
     for j in range(OWN):
         row = jnp.where(at >> 3 == j, jnp.broadcast_to(picks[j], shape), row)
     ylo, z, r = row >> 5, (row >> 2) & 7, row & 3
@@ -111,12 +117,15 @@
     return (((z * N_YHI + yhi) * N_YLO + ylo) * N_CORE + core) * OWN + r
 
 
-def attend_kernel(own_hbm, q_ref, kv1, kv2, kv3, out_ref, own, sem):
+def attend_kernel(own_hbm, q_ref, kv1, kv2, kv3, out_ref, own, info, sem):
     x, yhi, core = (lax.axis_index(a) for a in ("x", "yhi", "core"))
-    load = pltpu.make_async_copy(own_hbm.at[pl.ds(0, 2 * KEYS + INFO)], own, sem)
-    load.start()
+    words_load = pltpu.make_async_copy(own_hbm.at[pl.ds(2 * KEYS, INFO)], info, sem.at[0])
+    own_load = pltpu.make_async_copy(own_hbm.at[pl.ds(0, 2 * KEYS)], own, sem.at[1])
+    words_load.start()
+    own_load.start()
     kvs = [kv1, kv2, kv3, own]
     sources = [lax.rem(x + N_X - i, N_X) for i in (1, 2, 3, 0)]
+    suffix = (COM + BRA, OWN * SUF)
 
     def key(kv, at, count):
         return kv[pl.ds(at, count)]
@@ -126,34 +135,37 @@
 
     q = q_ref[...]
     scores = [score(q, key(kv, 0, COM)) for kv in kvs[:-1]]
-    load.wait()
-    scores.append(score(q, key(own, 0, COM)))
-    out, top, total = weigh(scores, values(0, COM))
-
-    info = own[pl.ds(2 * KEYS, INFO)].astype(F32).astype(jnp.int32)
-    words = [info[j : j + 1, 0:1] for j in range(3 * OWN)]
+
+    words_load.wait()
+    words = info[...].astype(F32).astype(jnp.int32)
+    words = [words[j : j + 1, 0:1] for j in range(3 * OWN)]
     picks = words[:OWN]
     lives = [16 * words[OWN + j] + words[2 * OWN + j] for j in range(OWN)]
     shape = (2 * PICKED, LINES)
-    select = lax.broadcasted_iota(jnp.int32, shape, 1) == picked_lines(picks, shape, 0)
+    select = lax.broadcasted_iota(jnp.int32, shape, 1) == picked_lines(picks, 0)
     q_sel = jnp.dot(select.astype(F32).astype(BF16), q, preferred_element_type=F32).astype(BF16)
-    scores = [score(q_sel[:PICKED], key(kv, COM, BRA)) for kv in kvs]
-    b_out, b_top, b_total = weigh(scores, values(COM, BRA))
 
     shape = (PICKED, OWN * SUF)
     q_row = lax.broadcasted_iota(jnp.int32, shape, 0) >> 3
-    slot = lax.broadcasted_iota(jnp.int32, shape, 1)
+    slot = lax.broadcasted_iota(jnp.int32, (1, OWN * SUF), 1)
     k_row, slot = slot >> 6, slot & (SUF - 1)
-    live = jnp.zeros(shape, jnp.int32)
+    live = jnp.zeros(k_row.shape, jnp.int32)
     for j in range(OWN):
-        live = jnp.where(k_row == j, jnp.broadcast_to(lives[j], shape), live)
+        live = jnp.where(k_row == j, jnp.broadcast_to(lives[j], live.shape), live)
     masks = []
     for source in sources:
         first = ((source * N_YHI + yhi) * N_CORE + core) * SUF
-        masks.append((q_row == k_row) & (slot + first < live))
-    suffix = (COM + BRA, OWN * SUF)
-    scores = [score(q_sel[PICKED:], key(kv, *suffix), mask) for kv, mask in zip(kvs, masks)]
-    s_out, s_top, s_total = weigh(scores, values(*suffix), masks)
+        masks.append(q_row == jnp.where(slot + first < live, k_row, -1))
+
+    b_scores = [score(q_sel[:PICKED], key(kv, COM, BRA)) for kv in kvs[:-1]]
+    s_scores = [score(q_sel[PICKED:], key(kv, *suffix), mask) for kv, mask in zip(kvs[:-1], masks)]
+    own_load.wait()
+    scores.append(score(q, key(own, 0, COM)))
+    b_scores.append(score(q_sel[:PICKED], key(own, COM, BRA)))
+    s_scores.append(score(q_sel[PICKED:], key(own, *suffix), masks[-1]))
+    out, top, total = weigh(scores, values(0, COM))
+    b_out, b_top, b_total = weigh(b_scores, values(COM, BRA))
+    s_out, s_top, s_total = weigh(s_scores, values(*suffix), masks)
 
     square = (2 * PICKED, 2 * PICKED)
     eye = lax.broadcasted_iota(jnp.int32, square, 0) == lax.broadcasted_iota(jnp.int32, square, 1)
@@ -163,7 +175,7 @@
         return jnp.sum(jnp.where(eye, col, 0.0), axis=0, keepdims=True)
 
     shape = (LINES, 2 * PICKED)
-    place_of = lax.broadcasted_iota(jnp.int32, shape, 0) == picked_lines(picks, shape, 1)
+    place_of = lax.broadcasted_iota(jnp.int32, shape, 0) == picked_lines(picks, 1)
     p_top = jnp.where(place_of, jnp.broadcast_to(across(b_top, s_top), shape), LOW)
     high = jnp.maximum(top, jnp.max(p_top, axis=1, keepdims=True))
     weight = jnp.where(place_of, jnp.exp2(p_top - high), 0.0)
@@ -231,35 +243,43 @@
     ]
     block = (2 * KEYS, HEAD_DIM)
     block = (2 * KEYS, HEAD_DIM)
-    packed = call(
+    q, *packed = call(
         pack_kernel,
-        [jax.ShapeDtypeStruct((OWN_ROOM, HEAD_DIM), BF16)]
+        [
+            jax.ShapeDtypeStruct((PEERS, OWN, HEAD_DIM), BF16),
+            jax.ShapeDtypeStruct((OWN_ROOM, HEAD_DIM), BF16),
+        ]
         + [jax.ShapeDtypeStruct(block, BF16)] * (N_X - 1),
-        [HBM] * 8,
+        [HBM] * 9,
         [
             pltpu.VMEM((2 * KEYS, width), BF16),
             pltpu.VMEM((N_X, *block), BF16),
             pltpu.VMEM((INFO, HEAD_DIM), BF16),
+            pltpu.VMEM((1, OWN, HEAD_DIM), BF16),
+            pltpu.VMEM((PEERS, OWN, HEAD_DIM), BF16),
             pltpu.SMEM((ROWS,), jnp.int32),
             pltpu.SMEM((OWN,), jnp.int32),
             pltpu.SMEM((2 * OWN,), jnp.int32),
-            pltpu.SemaphoreType.DMA((8,)),
+            pltpu.SemaphoreType.DMA((9,)),
             pltpu.SemaphoreType.DMA((N_X, 7)),
         ],
-        [HBM] * N_X,
+        [HBM] * (1 + N_X),
         PACK_LIMIT,
-    )(row_branch, suffix_len, *flat)
+    )(queries[None], row_branch, suffix_len, *flat)
     kvs = {i: turn(packed[i], "x", i) for i in (1, 3, 2)}
     kvs = [kvs[i] for i in range(1, N_X)]
 
-    q = jnp.broadcast_to(queries[None], (PEERS, OWN, HEAD_DIM))
     q = lax.all_to_all(q, PLANE, split_axis=0, concat_axis=0, tiled=True)
     q = q.reshape(LINES, HEAD_DIM)
     parts = call(
         attend_kernel,
         jax.ShapeDtypeStruct((PEERS * CHUNK, HEAD_DIM), F32),
         [HBM] + [VMEM] * 4,
-        [pltpu.VMEM((2 * KEYS + INFO, HEAD_DIM), BF16), pltpu.SemaphoreType.DMA],
+        [
+            pltpu.VMEM(block, BF16),
+            pltpu.VMEM((INFO, HEAD_DIM), BF16),
+            pltpu.SemaphoreType.DMA((2,)),
+        ],
     )(packed[0], q, *kvs)
     parts = parts.reshape(PEERS * CHUNK, 1, HEAD_DIM)
     parts = lax.all_to_all(parts, PLANE, split_axis=0, concat_axis=0, tiled=True)

time: 72.6 us -> 72.2 us (level)
  transfers between devices with their start and end apart: 3 -> 3, of which waited for: 0 -> 0; matrix products, arithmetic and copies ran while one was open for 1% -> 0% of each run, Pallas kernels for 0% -> 0%
where the time goes in v5:
time: 72.2 us; the launch traced here: 71.9 us
  blocking collectives  54.1 us (75%)
  starting transfers between devices  11.4 us (16%)
  Pallas kernels  6.29 us (9%)
    all_to_all x1, blocking collectives, local(): q = lax.all_to_all(q, PLANE, split_axis=0, concat_axis=0, tiled=True)  31.2 us
    all_to_all x1, blocking collectives, local(): lax.all_to_all(parts, PLANE, split_axis=0, concat_axis=0, tiled=True)  23 us
    ppermute x3, starting transfers between devices, turn(): lax.ppermute(value, axis, [(i, (i + step) % size) for i in range(size)])  11.4 us
    pallas_call x1, Pallas kernels, local(): call(attend_kernel, jax.ShapeDtypeStruct((PEERS * CHUNK, HEAD_DIM), F32),...  2.77 us
    pallas_call x1, Pallas kernels, local(): call(pack_kernel, [jax.ShapeDtypeStruct((PEERS, OWN, HEAD_DIM), BF16), ja...  2.75 us
  transfers between devices with their start and end apart: 3, of which 0 were waited for; matrix products, arithmetic and copies ran while one was open for 0% of the time, Pallas kernels for 0%

profile of v5, /device:TPU:1, one launch (start us, length us, event | category | flops | bytes accessed | tf_op | source)
XLA Modules:
  0.0 71.9 jit_solution(10218008161427777842)
XLA Ops:
  0.0 2.8 %shard_map.91 = (bf16[128,4,128]{2,1,0:T(4,128)(2,1)}, bf16[65536,128]{1,0:T(8,128)(2,1)}, bf16[2048,128]{1,0:T(8,128)(2,1)}, bf16[2048,128]{1,0:T(8,128)(2,1)}, bf16[2048,128]{1,0:T(8,128)(2,1)}) custom-call(bf16[1,4,128]{2,1,0:T(4,128)(2,1)} %bitcast.17, s32[64]{0:T(128)} %row_branch.1, s32[4]{0:T(128)} %suffix_len.1, bf16[256,512]{1,0:T(8,128)(2,1)} %ck.1, ...), custom_call_target="tpu_custom_call" | custom-call | tf_op jit(solution)/shard_map/pallas_call | solution.py:246
  2.8 3.9 %collective-permute-start = (bf16[2048,128]{1,0:T(8,128)(2,1)}, bf16[2048,128]{1,0:T(8,128)(2,1)S(1)}, u32[]{:S(2)}, u32[]{:S(2)}) collective-permute-start(bf16[2048,128]{1,0:T(8,128)(2,1)} %get-tuple-element.12), channel_id=1, source_target_pairs={{0,8},{8,16},{16,24},{24,0},{1,9},{9,17},{17,25},{25,1},{2,10},{10... | collective-permute-start | bytes 1572872 | tf_op jit(solution)/shard_map/ppermute | solution.py:225
  6.7 4.4 %collective-permute-start.1 = (bf16[2048,128]{1,0:T(8,128)(2,1)}, bf16[2048,128]{1,0:T(8,128)(2,1)S(1)}, u32[]{:S(2)}, u32[]{:S(2)}) collective-permute-start(bf16[2048,128]{1,0:T(8,128)(2,1)} %get-tuple-element.13), channel_id=1, source_target_pairs={{0,16},{8,24},{16,0},{24,8},{1,17},{9,25},{17,1},{25,9},{2,18},{10... | collective-permute-start | bytes 1572872 | tf_op jit(solution)/shard_map/ppermute | solution.py:225
  11.1 3.1 %collective-permute-start.2 = (bf16[2048,128]{1,0:T(8,128)(2,1)}, bf16[2048,128]{1,0:T(8,128)(2,1)S(1)}, u32[]{:S(2)}, u32[]{:S(2)}) collective-permute-start(bf16[2048,128]{1,0:T(8,128)(2,1)} %get-tuple-element.14), channel_id=1, source_target_pairs={{0,24},{8,0},{16,8},{24,16},{1,25},{9,1},{17,9},{25,17},{2,26},{10... | collective-permute-start | bytes 1572872 | tf_op jit(solution)/shard_map/ppermute | solution.py:225
  14.2 31.2 %all_to_all.10 = bf16[128,4,128]{2,1,0:T(4,128)(2,1)S(1)} all-to-all(bf16[128,4,128]{2,1,0:T(4,128)(2,1)} %get-tuple-element.11), channel_id=1, replica_groups=mesh['ylo'=2,'z'=8,'x'=4,'yhi'=4,'core'=2] {'z','yhi','ylo','core'}, dimensions={0} | all-to-all | bytes 262144 | tf_op jit(solution)/shard_map/all_to_all | solution.py:272
  45.3 0.0 collective-permute-done.kv1
  45.3 0.0 collective-permute-done.1.kv2
  45.3 0.0 collective-permute-done.2.kv3
  45.3 2.8 %shard_map.92 = f32[640,128]{1,0:T(8,128)S(1)} custom-call(bf16[65536,128]{1,0:T(8,128)(2,1)} %get-tuple-element.10.own_hbm, bf16[512,128]{1,0:T(8,128)(2,1)S(1)} %bitcast.12, bf16[2048,128]{1,0:T(8,128)(2,1)S(1)} %collective-permute-done.kv1, bf16[2048,128]{1,0:T(8,128)(2,1)S(1)} %collective-permute-done.1.kv2, bf16[2048,128]{1,0:T(8,128)(2,1)S(1)} %collective-permute-done.2.kv3), custom_call_target="tpu_custom_call" | custom-call | tf_op jit(solution)/shard_map/pallas_call | solution.py:274
  48.1 23.0 %all_to_all.11 = f32[640,1,128]{2,1,0:T(1,128)S(1)} all-to-all(f32[640,1,128]{2,1,0:T(1,128)S(1)} %bitcast.11), channel_id=1, replica_groups=mesh['ylo'=2,'z'=8,'x'=4,'yhi'=4,'core'=2] {'z','yhi','ylo','core'}, dimensions={0} | all-to-all | bytes 655360 | tf_op jit(solution)/shard_map/all_to_all | solution.py:285
  71.1 0.8 %shard_map.93 = bf16[4,128]{1,0:T(4,128)(2,1)} custom-call(f32[640,128]{1,0:T(8,128)S(1)} %bitcast.10), custom_call_target="tpu_custom_call" | custom-call | tf_op jit(solution)/shard_map/pallas_call | solution.py:287
Async XLA Ops:
  2.8 42.6 %collective-permute-start = (bf16[2048,128]{1,0:T(8,128)(2,1)}, bf16[2048,128]{1,0:T(8,128)(2,1)S(1)}, u32[]{:S(2)}, u32[]{:S(2)}) collective-permute-start(bf16[2048,128]{1,0:T(8,128)(2,1)} %get-tuple-element.12), channel_id=1, source_target_pairs={{0,8},{8,16},{16,24},{24,0},{1,9},{9,17},{17,25},{25,1},{2,10},{10... | collective-permute-start | bytes 1572872 | tf_op jit(solution)/shard_map/ppermute | solution.py:225
  6.7 38.6 %collective-permute-start.1 = (bf16[2048,128]{1,0:T(8,128)(2,1)}, bf16[2048,128]{1,0:T(8,128)(2,1)S(1)}, u32[]{:S(2)}, u32[]{:S(2)}) collective-permute-start(bf16[2048,128]{1,0:T(8,128)(2,1)} %get-tuple-element.13), channel_id=1, source_target_pairs={{0,16},{8,24},{16,0},{24,8},{1,17},{9,25},{17,1},{25,9},{2,18},{10... | collective-permute-start | bytes 1572872 | tf_op jit(solution)/shard_map/ppermute | solution.py:225
  11.1 34.3 %collective-permute-start.2 = (bf16[2048,128]{1,0:T(8,128)(2,1)}, bf16[2048,128]{1,0:T(8,128)(2,1)S(1)}, u32[]{:S(2)}, u32[]{:S(2)}) collective-permute-start(bf16[2048,128]{1,0:T(8,128)(2,1)} %get-tuple-element.14), channel_id=1, source_target_pairs={{0,24},{8,0},{16,8},{24,16},{1,25},{9,1},{17,9},{25,17},{2,26},{10... | collective-permute-start | bytes 1572872 | tf_op jit(solution)/shard_map/ppermute | solution.py:225

commit v6 on v5

--- a/solution.py
+++ b/solution.py
@@ -16,6 +16,7 @@
 N_X, N_YHI, N_CORE, N_YLO, N_Z = 4, 4, 2, 2, 8
 PLANE = ("z", "yhi", "ylo", "core")
 PEERS = N_Z * N_YHI * N_YLO * N_CORE
+STEPS = (2, 1, 3)
 ROWS = 64
 OWN = 4
 COM, BRA, SUF = 256, 512, 64
@@ -106,9 +107,9 @@
 
 
 def picked_lines(picks, axis):
-    shape = (2 * PICKED, 1) if axis == 0 else (1, 2 * PICKED)
+    shape = (2 * PICKED, 1) if axis == 0 else (1, 4 * PICKED)
     branch = lax.axis_index("ylo") * N_Z + lax.axis_index("z")
-    at = lax.broadcasted_iota(jnp.int32, shape, axis)
+    at = lax.broadcasted_iota(jnp.int32, shape, axis) & (2 * PICKED - 1)
     row = branch * OWN + ((at >> 3) & (OWN - 1))
     for j in range(OWN):
         row = jnp.where(at >> 3 == j, jnp.broadcast_to(picks[j], shape), row)
@@ -117,14 +118,14 @@
     return (((z * N_YHI + yhi) * N_YLO + ylo) * N_CORE + core) * OWN + r
 
 
-def attend_kernel(own_hbm, q_ref, kv1, kv2, kv3, out_ref, own, info, sem):
+def attend_kernel(own_hbm, q_ref, kv_a, kv_b, kv_c, out_ref, own, info, sem):
     x, yhi, core = (lax.axis_index(a) for a in ("x", "yhi", "core"))
     words_load = pltpu.make_async_copy(own_hbm.at[pl.ds(2 * KEYS, INFO)], info, sem.at[0])
     own_load = pltpu.make_async_copy(own_hbm.at[pl.ds(0, 2 * KEYS)], own, sem.at[1])
     words_load.start()
     own_load.start()
-    kvs = [kv1, kv2, kv3, own]
-    sources = [lax.rem(x + N_X - i, N_X) for i in (1, 2, 3, 0)]
+    kvs = [kv_a, kv_b, kv_c, own]
+    sources = [lax.rem(x + N_X - i, N_X) for i in (*STEPS, 0)]
     suffix = (COM + BRA, OWN * SUF)
 
     def key(kv, at, count):
@@ -167,23 +168,32 @@
     b_out, b_top, b_total = weigh(b_scores, values(COM, BRA))
     s_out, s_top, s_total = weigh(s_scores, values(*suffix), masks)
 
-    square = (2 * PICKED, 2 * PICKED)
-    eye = lax.broadcasted_iota(jnp.int32, square, 0) == lax.broadcasted_iota(jnp.int32, square, 1)
+    square = (2 * PICKED, 4 * PICKED)
+    column = lax.broadcasted_iota(jnp.int32, square, 1)
+    eye = lax.broadcasted_iota(jnp.int32, square, 0) == column & (2 * PICKED - 1)
 
     def across(a, b):
         col = jnp.broadcast_to(jnp.concatenate([a, b], axis=0), square)
         return jnp.sum(jnp.where(eye, col, 0.0), axis=0, keepdims=True)
 
-    shape = (LINES, 2 * PICKED)
+    shape = (LINES, 4 * PICKED)
     place_of = lax.broadcasted_iota(jnp.int32, shape, 0) == picked_lines(picks, 1)
+    first = lax.broadcasted_iota(jnp.int32, shape, 1) < 2 * PICKED
     p_top = jnp.where(place_of, jnp.broadcast_to(across(b_top, s_top), shape), LOW)
     high = jnp.maximum(top, jnp.max(p_top, axis=1, keepdims=True))
     weight = jnp.where(place_of, jnp.exp2(p_top - high), 0.0)
     scale = jnp.exp2(top - high)
+    near = weight.astype(BF16).astype(F32)
+    weights = [jnp.where(first, near, weight - near), jnp.where(first, near, 0.0)]
     parts = jnp.concatenate([b_out, s_out], axis=0)
+    p_near = parts.astype(BF16).astype(F32)
+    parts = [p_near, p_near, parts - p_near, jnp.zeros_like(parts)]
     out = out * scale + jnp.dot(
-        weight, parts, precision=lax.Precision.HIGHEST, preferred_element_type=F32
+        jnp.concatenate(weights, axis=1).astype(BF16),
+        jnp.concatenate(parts, axis=0).astype(BF16),
+        preferred_element_type=F32,
     )
+    weight = jnp.where(first, weight, 0.0)
     total = total * scale + jnp.sum(weight * across(b_total, s_total), axis=1, keepdims=True)
 
     shape = (LINES, HEAD_DIM)
@@ -266,8 +276,7 @@
         [HBM] * (1 + N_X),
         PACK_LIMIT,
     )(queries[None], row_branch, suffix_len, *flat)
-    kvs = {i: turn(packed[i], "x", i) for i in (1, 3, 2)}
-    kvs = [kvs[i] for i in range(1, N_X)]
+    kvs = [turn(packed[i], "x", i) for i in STEPS]
 
     q = lax.all_to_all(q, PLANE, split_axis=0, concat_axis=0, tiled=True)
     q = q.reshape(LINES, HEAD_DIM)

time: 72.2 us -> 71.3 us (0.988)
  blocking collectives: 54.1 us -> 52.8 us
    all_to_all x1, blocking collectives: 23 us -> 21.6 us  [local(): lax.all_to_all(parts, PLANE, split_axis=0, concat_axis=0, tiled=True)]
where the time goes in v6:
time: 71.3 us; the launch traced here: 71 us
  blocking collectives  52.8 us (74%)
  starting transfers between devices  12 us (17%)
  Pallas kernels  6.16 us (9%)
    all_to_all x1, blocking collectives, local(): q = lax.all_to_all(q, PLANE, split_axis=0, concat_axis=0, tiled=True)  31.2 us
    all_to_all x1, blocking collectives, local(): lax.all_to_all(parts, PLANE, split_axis=0, concat_axis=0, tiled=True)  21.6 us
    ppermute x3, starting transfers between devices, turn(): lax.ppermute(value, axis, [(i, (i + step) % size) for i in range(size)])  12 us
    pallas_call x1, Pallas kernels, local(): call(pack_kernel, [jax.ShapeDtypeStruct((PEERS, OWN, HEAD_DIM), BF16), ja...  2.75 us
    pallas_call x1, Pallas kernels, local(): call(attend_kernel, jax.ShapeDtypeStruct((PEERS * CHUNK, HEAD_DIM), F32),...  2.64 us
  transfers between devices with their start and end apart: 3, of which 0 were waited for; matrix products, arithmetic and copies ran while one was open for 0% of the time, Pallas kernels for 0%

profile of v6, /device:TPU:1, one launch (start us, length us, event | category | flops | bytes accessed | tf_op | source)
XLA Modules:
  0.0 71.0 jit_solution(14962340674313358241)
XLA Ops:
  0.0 2.8 %shard_map.91 = (bf16[128,4,128]{2,1,0:T(4,128)(2,1)}, bf16[65536,128]{1,0:T(8,128)(2,1)}, bf16[2048,128]{1,0:T(8,128)(2,1)}, bf16[2048,128]{1,0:T(8,128)(2,1)}, bf16[2048,128]{1,0:T(8,128)(2,1)}) custom-call(bf16[1,4,128]{2,1,0:T(4,128)(2,1)} %bitcast.17, s32[64]{0:T(128)} %row_branch.1, s32[4]{0:T(128)} %suffix_len.1, bf16[256,512]{1,0:T(8,128)(2,1)} %ck.1, ...), custom_call_target="tpu_custom_call" | custom-call | tf_op jit(solution)/shard_map/pallas_call | solution.py:256
  2.8 5.5 %collective-permute-start = (bf16[2048,128]{1,0:T(8,128)(2,1)}, bf16[2048,128]{1,0:T(8,128)(2,1)S(1)}, u32[]{:S(2)}, u32[]{:S(2)}) collective-permute-start(bf16[2048,128]{1,0:T(8,128)(2,1)} %get-tuple-element.12), channel_id=1, source_target_pairs={{0,16},{8,24},{16,0},{24,8},{1,17},{9,25},{17,1},{25,9},{2,18},{10... | collective-permute-start | bytes 1572872 | tf_op jit(solution)/shard_map/ppermute | solution.py:235
  8.3 2.2 %collective-permute-start.1 = (bf16[2048,128]{1,0:T(8,128)(2,1)}, bf16[2048,128]{1,0:T(8,128)(2,1)S(1)}, u32[]{:S(2)}, u32[]{:S(2)}) collective-permute-start(bf16[2048,128]{1,0:T(8,128)(2,1)} %get-tuple-element.13), channel_id=1, source_target_pairs={{0,8},{8,16},{16,24},{24,0},{1,9},{9,17},{17,25},{25,1},{2,10},{10... | collective-permute-start | bytes 1572872 | tf_op jit(solution)/shard_map/ppermute | solution.py:235
  10.5 4.3 %collective-permute-start.2 = (bf16[2048,128]{1,0:T(8,128)(2,1)}, bf16[2048,128]{1,0:T(8,128)(2,1)S(1)}, u32[]{:S(2)}, u32[]{:S(2)}) collective-permute-start(bf16[2048,128]{1,0:T(8,128)(2,1)} %get-tuple-element.14), channel_id=1, source_target_pairs={{0,24},{8,0},{16,8},{24,16},{1,25},{9,1},{17,9},{25,17},{2,26},{10... | collective-permute-start | bytes 1572872 | tf_op jit(solution)/shard_map/ppermute | solution.py:235
  14.8 31.2 %all_to_all.10 = bf16[128,4,128]{2,1,0:T(4,128)(2,1)S(1)} all-to-all(bf16[128,4,128]{2,1,0:T(4,128)(2,1)} %get-tuple-element.11), channel_id=1, replica_groups=mesh['ylo'=2,'z'=8,'x'=4,'yhi'=4,'core'=2] {'z','yhi','ylo','core'}, dimensions={0} | all-to-all | bytes 262144 | tf_op jit(solution)/shard_map/all_to_all | solution.py:281
  45.9 0.0 collective-permute-done.kv_a
  45.9 0.0 collective-permute-done.1.kv_b
  45.9 0.0 collective-permute-done.2.kv_c
  45.9 2.6 %shard_map.92 = f32[640,128]{1,0:T(8,128)S(1)} custom-call(bf16[65536,128]{1,0:T(8,128)(2,1)} %get-tuple-element.10.own_hbm, bf16[512,128]{1,0:T(8,128)(2,1)S(1)} %bitcast.12, bf16[2048,128]{1,0:T(8,128)(2,1)S(1)} %collective-permute-done.kv_a, bf16[2048,128]{1,0:T(8,128)(2,1)S(1)} %collective-permute-done.1.kv_b, ...), custom_call_target="tpu_custom_call" | custom-call | tf_op jit(solution)/shard_map/pallas_call | solution.py:283
  48.6 21.6 %all_to_all.11 = f32[640,1,128]{2,1,0:T(1,128)S(1)} all-to-all(f32[640,1,128]{2,1,0:T(1,128)S(1)} %bitcast.11), channel_id=1, replica_groups=mesh['ylo'=2,'z'=8,'x'=4,'yhi'=4,'core'=2] {'z','yhi','ylo','core'}, dimensions={0} | all-to-all | bytes 655360 | tf_op jit(solution)/shard_map/all_to_all | solution.py:294
  70.2 0.8 %shard_map.93 = bf16[4,128]{1,0:T(4,128)(2,1)} custom-call(f32[640,128]{1,0:T(8,128)S(1)} %bitcast.10), custom_call_target="tpu_custom_call" | custom-call | tf_op jit(solution)/shard_map/pallas_call | solution.py:296
Async XLA Ops:
  2.8 43.2 %collective-permute-start = (bf16[2048,128]{1,0:T(8,128)(2,1)}, bf16[2048,128]{1,0:T(8,128)(2,1)S(1)}, u32[]{:S(2)}, u32[]{:S(2)}) collective-permute-start(bf16[2048,128]{1,0:T(8,128)(2,1)} %get-tuple-element.12), channel_id=1, source_target_pairs={{0,16},{8,24},{16,0},{24,8},{1,17},{9,25},{17,1},{25,9},{2,18},{10... | collective-permute-start | bytes 1572872 | tf_op jit(solution)/shard_map/ppermute | solution.py:235
  8.3 37.7 %collective-permute-start.1 = (bf16[2048,128]{1,0:T(8,128)(2,1)}, bf16[2048,128]{1,0:T(8,128)(2,1)S(1)}, u32[]{:S(2)}, u32[]{:S(2)}) collective-permute-start(bf16[2048,128]{1,0:T(8,128)(2,1)} %get-tuple-element.13), channel_id=1, source_target_pairs={{0,8},{8,16},{16,24},{24,0},{1,9},{9,17},{17,25},{25,1},{2,10},{10... | collective-permute-start | bytes 1572872 | tf_op jit(solution)/shard_map/ppermute | solution.py:235
  10.5 35.5 %collective-permute-start.2 = (bf16[2048,128]{1,0:T(8,128)(2,1)}, bf16[2048,128]{1,0:T(8,128)(2,1)S(1)}, u32[]{:S(2)}, u32[]{:S(2)}) collective-permute-start(bf16[2048,128]{1,0:T(8,128)(2,1)} %get-tuple-element.14), channel_id=1, source_target_pairs={{0,24},{8,0},{16,8},{24,16},{1,25},{9,1},{17,9},{25,17},{2,26},{10... | collective-permute-start | bytes 1572872 | tf_op jit(solution)/shard_map/ppermute | solution.py:235

commit v7 on v6

--- a/solution.py
+++ b/solution.py
@@ -25,7 +25,8 @@
 PICKED = OWN * GROUP
 INFO = 16
 OWN_ROOM = 1 << 16
-CHUNK = OWN + 1
+CHUNK = OWN + 2
+TOP_AT, TOTAL_AT, POWER_AT = (0, 4, 8), (16, 20, 24), 32
 LOW = -1e30
 F32 = jnp.float32
 BF16 = jnp.bfloat16
@@ -196,26 +197,40 @@
     weight = jnp.where(first, weight, 0.0)
     total = total * scale + jnp.sum(weight * across(b_total, s_total), axis=1, keepdims=True)
 
+    power = jnp.ceil(jnp.log(jnp.max(jnp.abs(out), axis=1, keepdims=True)) * math.log2(math.e))
+    power = jnp.clip(power, -120.0, 120.0)
+    out = out * jnp.exp2(-power)
     shape = (LINES, HEAD_DIM)
-    lane = lax.broadcasted_iota(jnp.int32, shape, 1)
     r = lax.broadcasted_iota(jnp.int32, shape, 0) & (OWN - 1)
-    stat = jnp.where(lane == r, high, 0.0) + jnp.where(lane == r + OWN, total, 0.0)
+    lane = lax.broadcasted_iota(jnp.int32, shape, 1) - r
+    stat = jnp.where(lane == POWER_AT, power, 0.0)
+    for value, lanes in ((high, TOP_AT), (total, TOTAL_AT)):
+        for at in lanes:
+            piece = value.astype(BF16).astype(F32)
+            stat = jnp.where(lane == at, piece, stat)
+            value = value - piece
     stat = sum(pltpu.roll(stat, i, 0) for i in range(1, OWN)) + stat
     for c in range(PEERS):
         out_ref[pl.ds(c * CHUNK, OWN)] = out[c * OWN : (c + 1) * OWN]
-        out_ref[pl.ds(c * CHUNK + OWN, 1)] = stat[(c + 1) * OWN - 1 : (c + 1) * OWN]
+        out_ref[pl.ds(c * CHUNK + OWN, 2)] = stat[(c + 1) * OWN - 2 : (c + 1) * OWN]
 
 
 def merge_kernel(parts, out):
-    stat = parts[pl.ds(OWN, PEERS, stride=CHUNK), :]
-    high = jnp.max(stat, axis=0, keepdims=True)
-    weight = jnp.exp2(jnp.minimum(stat - high, 0.0))
-    total = jnp.sum(pltpu.roll(weight, OWN, 1) * stat, axis=0, keepdims=True)
+    stat = parts[pl.ds(CHUNK - 1, PEERS, stride=CHUNK), :]
+
+    def value(*lanes):
+        return sum(pltpu.roll(stat, (HEAD_DIM - at) % HEAD_DIM, 1) for at in lanes)
+
+    top = value(*TOP_AT)
+    high = jnp.max(top, axis=0, keepdims=True)
+    weight = jnp.exp2(jnp.minimum(top - high, 0.0))
+    total = jnp.sum(weight * value(*TOTAL_AT), axis=0, keepdims=True)
+    weight = weight * jnp.exp2(value(POWER_AT))
     rows = []
     for r in range(OWN):
         part = parts[pl.ds(r, PEERS, stride=CHUNK), :]
         got = jnp.sum(part * weight[:, r : r + 1], axis=0, keepdims=True)
-        rows.append(got / total[:, OWN + r : OWN + r + 1])
+        rows.append(got / total[:, r : r + 1])
     out[...] = jnp.concatenate(rows, axis=0).astype(BF16)
 
 
@@ -290,9 +305,9 @@
             pltpu.SemaphoreType.DMA((2,)),
         ],
     )(packed[0], q, *kvs)
-    parts = parts.reshape(PEERS * CHUNK, 1, HEAD_DIM)
+    parts = parts.astype(jnp.float16).reshape(PEERS * CHUNK // 2, 2, HEAD_DIM)
     parts = lax.all_to_all(parts, PLANE, split_axis=0, concat_axis=0, tiled=True)
-    parts = parts.reshape(PEERS * CHUNK, HEAD_DIM)
+    parts = parts.reshape(PEERS * CHUNK, HEAD_DIM).astype(F32)
     return call(merge_kernel, jax.ShapeDtypeStruct((OWN, HEAD_DIM), BF16), [VMEM])(parts)
 
 

time: 71.3 us -> 69.2 us (0.971)
  blocking collectives: 52.8 us -> 50.2 us
    all_to_all x1, blocking collectives: 21.6 us -> 19 us  [local(): lax.all_to_all(parts, PLANE, split_axis=0, concat_axis=0, tiled=True)]
where the time goes in v7:
time: 69.2 us; the launch traced here: 68.9 us
  blocking collectives  50.2 us (73%)
  starting transfers between devices  12 us (17%)
  Pallas kernels  6.6 us (10%)
    all_to_all x1, blocking collectives, local(): q = lax.all_to_all(q, PLANE, split_axis=0, concat_axis=0, tiled=True)  31.2 us
    all_to_all x1, blocking collectives, local(): lax.all_to_all(parts, PLANE, split_axis=0, concat_axis=0, tiled=True)  19 us
    ppermute x3, starting transfers between devices, turn(): lax.ppermute(value, axis, [(i, (i + step) % size) for i in range(size)])  12 us
    pallas_call x1, Pallas kernels, local(): call(attend_kernel, jax.ShapeDtypeStruct((PEERS * CHUNK, HEAD_DIM), F32),...  2.96 us
    pallas_call x1, Pallas kernels, local(): call(pack_kernel, [jax.ShapeDtypeStruct((PEERS, OWN, HEAD_DIM), BF16), ja...  2.75 us
  transfers between devices with their start and end apart: 3, of which 0 were waited for; matrix products, arithmetic and copies ran while one was open for 0% of the time, Pallas kernels for 0%

profile of v7, /device:TPU:1, one launch (start us, length us, event | category | flops | bytes accessed | tf_op | source)
XLA Modules:
  0.0 68.9 jit_solution(7797700659083097305)
XLA Ops:
  0.0 2.8 %shard_map.91 = (bf16[128,4,128]{2,1,0:T(4,128)(2,1)}, bf16[65536,128]{1,0:T(8,128)(2,1)}, bf16[2048,128]{1,0:T(8,128)(2,1)}, bf16[2048,128]{1,0:T(8,128)(2,1)}, bf16[2048,128]{1,0:T(8,128)(2,1)}) custom-call(bf16[1,4,128]{2,1,0:T(4,128)(2,1)} %bitcast.16, s32[64]{0:T(128)} %row_branch.1, s32[4]{0:T(128)} %suffix_len.1, bf16[256,512]{1,0:T(8,128)(2,1)} %ck.1, ...), custom_call_target="tpu_custom_call" | custom-call | tf_op jit(solution)/shard_map/pallas_call | solution.py:271
  2.8 5.5 %collective-permute-start = (bf16[2048,128]{1,0:T(8,128)(2,1)}, bf16[2048,128]{1,0:T(8,128)(2,1)S(1)}, u32[]{:S(2)}, u32[]{:S(2)}) collective-permute-start(bf16[2048,128]{1,0:T(8,128)(2,1)} %get-tuple-element.12), channel_id=1, source_target_pairs={{0,16},{8,24},{16,0},{24,8},{1,17},{9,25},{17,1},{25,9},{2,18},{10... | collective-permute-start | bytes 1572872 | tf_op jit(solution)/shard_map/ppermute | solution.py:250
  8.3 2.2 %collective-permute-start.1 = (bf16[2048,128]{1,0:T(8,128)(2,1)}, bf16[2048,128]{1,0:T(8,128)(2,1)S(1)}, u32[]{:S(2)}, u32[]{:S(2)}) collective-permute-start(bf16[2048,128]{1,0:T(8,128)(2,1)} %get-tuple-element.13), channel_id=1, source_target_pairs={{0,8},{8,16},{16,24},{24,0},{1,9},{9,17},{17,25},{25,1},{2,10},{10... | collective-permute-start | bytes 1572872 | tf_op jit(solution)/shard_map/ppermute | solution.py:250
  10.5 4.3 %collective-permute-start.2 = (bf16[2048,128]{1,0:T(8,128)(2,1)}, bf16[2048,128]{1,0:T(8,128)(2,1)S(1)}, u32[]{:S(2)}, u32[]{:S(2)}) collective-permute-start(bf16[2048,128]{1,0:T(8,128)(2,1)} %get-tuple-element.14), channel_id=1, source_target_pairs={{0,24},{8,0},{16,8},{24,16},{1,25},{9,1},{17,9},{25,17},{2,26},{10... | collective-permute-start | bytes 1572872 | tf_op jit(solution)/shard_map/ppermute | solution.py:250
  14.8 31.2 %all_to_all.10 = bf16[128,4,128]{2,1,0:T(4,128)(2,1)S(1)} all-to-all(bf16[128,4,128]{2,1,0:T(4,128)(2,1)} %get-tuple-element.11), channel_id=1, replica_groups=mesh['ylo'=2,'z'=8,'x'=4,'yhi'=4,'core'=2] {'z','yhi','ylo','core'}, dimensions={0} | all-to-all | bytes 262144 | tf_op jit(solution)/shard_map/all_to_all | solution.py:296
  45.9 0.0 collective-permute-done.kv_a
  45.9 0.0 collective-permute-done.1.kv_b
  45.9 0.0 collective-permute-done.2.kv_c
  45.9 3.0 %shard_map.92 = f32[768,128]{1,0:T(8,128)S(1)} custom-call(bf16[65536,128]{1,0:T(8,128)(2,1)} %get-tuple-element.10.own_hbm, bf16[512,128]{1,0:T(8,128)(2,1)S(1)} %bitcast.9, bf16[2048,128]{1,0:T(8,128)(2,1)S(1)} %collective-permute-done.kv_a, bf16[2048,128]{1,0:T(8,128)(2,1)S(1)} %collective-permute-done.1.kv_b, ...), custom_call_target="tpu_custom_call" | custom-call | tf_op jit(solution)/shard_map/pallas_call | solution.py:298
  49.0 19.0 %all_to_all.11 = f16[384,2,128]{2,1,0:T(2,128)(2,1)S(1)} all-to-all(f16[384,2,128]{2,1,0:T(2,128)(2,1)S(1)} %bitcast.10), channel_id=1, replica_groups=mesh['ylo'=2,'z'=8,'x'=4,'yhi'=4,'core'=2] {'z','yhi','ylo','core'}, dimensions={0} | all-to-all | bytes 393216 | tf_op jit(solution)/shard_map/all_to_all | solution.py:309
  68.0 0.9 %shard_map.93 = bf16[4,128]{1,0:T(4,128)(2,1)} custom-call(f32[768,128]{1,0:T(8,128)S(1)} %convert.1.parts), custom_call_target="tpu_custom_call" | custom-call | tf_op jit(solution)/shard_map/pallas_call | solution.py:311
  (2 shorter events, 0.1 us)
Async XLA Ops:
  2.8 43.2 %collective-permute-start = (bf16[2048,128]{1,0:T(8,128)(2,1)}, bf16[2048,128]{1,0:T(8,128)(2,1)S(1)}, u32[]{:S(2)}, u32[]{:S(2)}) collective-permute-start(bf16[2048,128]{1,0:T(8,128)(2,1)} %get-tuple-element.12), channel_id=1, source_target_pairs={{0,16},{8,24},{16,0},{24,8},{1,17},{9,25},{17,1},{25,9},{2,18},{10... | collective-permute-start | bytes 1572872 | tf_op jit(solution)/shard_map/ppermute | solution.py:250
  8.3 37.7 %collective-permute-start.1 = (bf16[2048,128]{1,0:T(8,128)(2,1)}, bf16[2048,128]{1,0:T(8,128)(2,1)S(1)}, u32[]{:S(2)}, u32[]{:S(2)}) collective-permute-start(bf16[2048,128]{1,0:T(8,128)(2,1)} %get-tuple-element.13), channel_id=1, source_target_pairs={{0,8},{8,16},{16,24},{24,0},{1,9},{9,17},{17,25},{25,1},{2,10},{10... | collective-permute-start | bytes 1572872 | tf_op jit(solution)/shard_map/ppermute | solution.py:250
  10.5 35.5 %collective-permute-start.2 = (bf16[2048,128]{1,0:T(8,128)(2,1)}, bf16[2048,128]{1,0:T(8,128)(2,1)S(1)}, u32[]{:S(2)}, u32[]{:S(2)}) collective-permute-start(bf16[2048,128]{1,0:T(8,128)(2,1)} %get-tuple-element.14), channel_id=1, source_target_pairs={{0,24},{8,0},{16,8},{24,16},{1,25},{9,1},{17,9},{25,17},{2,26},{10... | collective-permute-start | bytes 1572872 | tf_op jit(solution)/shard_map/ppermute | solution.py:250

commit v8 on v7

--- a/solution.py
+++ b/solution.py
@@ -14,9 +14,9 @@
 GROUP = HEADS // KV_HEADS
 HEAD_DIM = 128
 N_X, N_YHI, N_CORE, N_YLO, N_Z = 4, 4, 2, 2, 8
-PLANE = ("z", "yhi", "ylo", "core")
+PLANE = ("yhi", "ylo", "z", "core")
 PEERS = N_Z * N_YHI * N_YLO * N_CORE
-STEPS = (2, 1, 3)
+STEPS = (2, 3, 1)
 ROWS = 64
 OWN = 4
 COM, BRA, SUF = 256, 512, 64
@@ -114,9 +114,12 @@
     row = branch * OWN + ((at >> 3) & (OWN - 1))
     for j in range(OWN):
         row = jnp.where(at >> 3 == j, jnp.broadcast_to(picks[j], shape), row)
-    ylo, z, r = row >> 5, (row >> 2) & 7, row & 3
-    yhi, core = (at >> 1) & 3, at & 1
-    return (((z * N_YHI + yhi) * N_YLO + ylo) * N_CORE + core) * OWN + r
+    place = {"ylo": row >> 5, "z": (row >> 2) & 7, "yhi": (at >> 1) & 3, "core": at & 1}
+    size = {"ylo": N_YLO, "z": N_Z, "yhi": N_YHI, "core": N_CORE}
+    line = 0
+    for axis_name in PLANE:
+        line = line * size[axis_name] + place[axis_name]
+    return line * OWN + (row & 3)
 
 
 def attend_kernel(own_hbm, q_ref, kv_a, kv_b, kv_c, out_ref, own, info, sem):

time: 69.2 us -> 67.6 us (0.977)
  starting transfers between devices: 12 us -> 10.8 us
    ppermute x3, starting transfers between devices: 12 us -> 10.8 us  [turn(): lax.ppermute(value, axis, [(i, (i + step) % size) for i in range(size)])]
where the time goes in v8:
time: 67.6 us; the launch traced here: 67.3 us
  blocking collectives  49.8 us (74%)
  starting transfers between devices  10.8 us (16%)
  Pallas kernels  6.61 us (10%)
    all_to_all x1, blocking collectives, local(): q = lax.all_to_all(q, PLANE, split_axis=0, concat_axis=0, tiled=True)  30.6 us
    all_to_all x1, blocking collectives, local(): lax.all_to_all(parts, PLANE, split_axis=0, concat_axis=0, tiled=True)  19.2 us
    ppermute x3, starting transfers between devices, turn(): lax.ppermute(value, axis, [(i, (i + step) % size) for i in range(size)])  10.8 us
    pallas_call x1, Pallas kernels, local(): call(attend_kernel, jax.ShapeDtypeStruct((PEERS * CHUNK, HEAD_DIM), F32),...  2.97 us
    pallas_call x1, Pallas kernels, local(): call(pack_kernel, [jax.ShapeDtypeStruct((PEERS, OWN, HEAD_DIM), BF16), ja...  2.75 us
  transfers between devices with their start and end apart: 3, of which 0 were waited for; matrix products, arithmetic and copies ran while one was open for 0% of the time, Pallas kernels for 0%

profile of v8, /device:TPU:1, one launch (start us, length us, event | category | flops | bytes accessed | tf_op | source)
XLA Modules:
  0.0 67.3 jit_solution(3206237019599612005)
XLA Ops:
  0.0 2.8 %shard_map.91 = (bf16[128,4,128]{2,1,0:T(4,128)(2,1)}, bf16[65536,128]{1,0:T(8,128)(2,1)}, bf16[2048,128]{1,0:T(8,128)(2,1)}, bf16[2048,128]{1,0:T(8,128)(2,1)}, bf16[2048,128]{1,0:T(8,128)(2,1)}) custom-call(bf16[1,4,128]{2,1,0:T(4,128)(2,1)} %bitcast.16, s32[64]{0:T(128)} %row_branch.1, s32[4]{0:T(128)} %suffix_len.1, bf16[256,512]{1,0:T(8,128)(2,1)} %ck.1, ...), custom_call_target="tpu_custom_call" | custom-call | tf_op jit(solution)/shard_map/pallas_call | solution.py:274
  2.8 5.5 %collective-permute-start = (bf16[2048,128]{1,0:T(8,128)(2,1)}, bf16[2048,128]{1,0:T(8,128)(2,1)S(1)}, u32[]{:S(2)}, u32[]{:S(2)}) collective-permute-start(bf16[2048,128]{1,0:T(8,128)(2,1)} %get-tuple-element.12), channel_id=1, source_target_pairs={{0,16},{8,24},{16,0},{24,8},{1,17},{9,25},{17,1},{25,9},{2,18},{10... | collective-permute-start | bytes 1572872 | tf_op jit(solution)/shard_map/ppermute | solution.py:253
  8.3 2.8 %collective-permute-start.1 = (bf16[2048,128]{1,0:T(8,128)(2,1)}, bf16[2048,128]{1,0:T(8,128)(2,1)S(1)}, u32[]{:S(2)}, u32[]{:S(2)}) collective-permute-start(bf16[2048,128]{1,0:T(8,128)(2,1)} %get-tuple-element.13), channel_id=1, source_target_pairs={{0,24},{8,0},{16,8},{24,16},{1,25},{9,1},{17,9},{25,17},{2,26},{10... | collective-permute-start | bytes 1572872 | tf_op jit(solution)/shard_map/ppermute | solution.py:253
  11.0 2.5 %collective-permute-start.2 = (bf16[2048,128]{1,0:T(8,128)(2,1)}, bf16[2048,128]{1,0:T(8,128)(2,1)S(1)}, u32[]{:S(2)}, u32[]{:S(2)}) collective-permute-start(bf16[2048,128]{1,0:T(8,128)(2,1)} %get-tuple-element.14), channel_id=1, source_target_pairs={{0,8},{8,16},{16,24},{24,0},{1,9},{9,17},{17,25},{25,1},{2,10},{10... | collective-permute-start | bytes 1572872 | tf_op jit(solution)/shard_map/ppermute | solution.py:253
  13.5 30.6 %all_to_all.10 = bf16[128,4,128]{2,1,0:T(4,128)(2,1)S(1)} all-to-all(bf16[128,4,128]{2,1,0:T(4,128)(2,1)} %get-tuple-element.11), channel_id=1, replica_groups=mesh['ylo'=2,'z'=8,'x'=4,'yhi'=4,'core'=2] {'yhi','ylo','z','core'}, dimensions={0} | all-to-all | bytes 262144 | tf_op jit(solution)/shard_map/all_to_all | solution.py:299
  44.1 0.0 collective-permute-done.kv_a
  44.1 0.0 collective-permute-done.1.kv_b
  44.2 0.0 collective-permute-done.2.kv_c
  44.2 3.0 %shard_map.92 = f32[768,128]{1,0:T(8,128)S(1)} custom-call(bf16[65536,128]{1,0:T(8,128)(2,1)} %get-tuple-element.10.own_hbm, bf16[512,128]{1,0:T(8,128)(2,1)S(1)} %bitcast.9, bf16[2048,128]{1,0:T(8,128)(2,1)S(1)} %collective-permute-done.kv_a, bf16[2048,128]{1,0:T(8,128)(2,1)S(1)} %collective-permute-done.1.kv_b, ...), custom_call_target="tpu_custom_call" | custom-call | tf_op jit(solution)/shard_map/pallas_call | solution.py:301
  47.2 19.2 %all_to_all.11 = f16[384,2,128]{2,1,0:T(2,128)(2,1)S(1)} all-to-all(f16[384,2,128]{2,1,0:T(2,128)(2,1)S(1)} %bitcast.10), channel_id=1, replica_groups=mesh['ylo'=2,'z'=8,'x'=4,'yhi'=4,'core'=2] {'yhi','ylo','z','core'}, dimensions={0} | all-to-all | bytes 393216 | tf_op jit(solution)/shard_map/all_to_all | solution.py:312
  66.4 0.9 %shard_map.93 = bf16[4,128]{1,0:T(4,128)(2,1)} custom-call(f32[768,128]{1,0:T(8,128)S(1)} %convert.1.parts), custom_call_target="tpu_custom_call" | custom-call | tf_op jit(solution)/shard_map/pallas_call | solution.py:314
  (2 shorter events, 0.1 us)
Async XLA Ops:
  2.8 41.4 %collective-permute-start = (bf16[2048,128]{1,0:T(8,128)(2,1)}, bf16[2048,128]{1,0:T(8,128)(2,1)S(1)}, u32[]{:S(2)}, u32[]{:S(2)}) collective-permute-start(bf16[2048,128]{1,0:T(8,128)(2,1)} %get-tuple-element.12), channel_id=1, source_target_pairs={{0,16},{8,24},{16,0},{24,8},{1,17},{9,25},{17,1},{25,9},{2,18},{10... | collective-permute-start | bytes 1572872 | tf_op jit(solution)/shard_map/ppermute | solution.py:253
  8.3 35.9 %collective-permute-start.1 = (bf16[2048,128]{1,0:T(8,128)(2,1)}, bf16[2048,128]{1,0:T(8,128)(2,1)S(1)}, u32[]{:S(2)}, u32[]{:S(2)}) collective-permute-start(bf16[2048,128]{1,0:T(8,128)(2,1)} %get-tuple-element.13), channel_id=1, source_target_pairs={{0,24},{8,0},{16,8},{24,16},{1,25},{9,1},{17,9},{25,17},{2,26},{10... | collective-permute-start | bytes 1572872 | tf_op jit(solution)/shard_map/ppermute | solution.py:253
  11.0 33.1 %collective-permute-start.2 = (bf16[2048,128]{1,0:T(8,128)(2,1)}, bf16[2048,128]{1,0:T(8,128)(2,1)S(1)}, u32[]{:S(2)}, u32[]{:S(2)}) collective-permute-start(bf16[2048,128]{1,0:T(8,128)(2,1)} %get-tuple-element.14), channel_id=1, source_target_pairs={{0,8},{8,16},{16,24},{24,0},{1,9},{9,17},{17,25},{25,1},{2,10},{10... | collective-permute-start | bytes 1572872 | tf_op jit(solution)/shard_map/ppermute | solution.py:253

commit v9 on v8

--- a/solution.py
+++ b/solution.py
@@ -90,7 +90,7 @@
 
 
 def score(q, key, mask=None):
-    s = lax.dot_general(q, key, (((1,), (1,)), ((), ())), preferred_element_type=F32) * SCALE
+    s = lax.dot_general(q, key, (((1,), (1,)), ((), ())), preferred_element_type=F32)
     return s if mask is None else jnp.where(mask, s, LOW)
 
 
@@ -98,13 +98,13 @@
     top = jnp.max(functools.reduce(jnp.maximum, scores), axis=1, keepdims=True)
     total = out = None
     for i, (s, value) in enumerate(zip(scores, values)):
-        w = jnp.exp2(s - top)
+        w = jnp.exp2((s - top) * SCALE)
         if masks is not None:
             w = jnp.where(masks[i], w, 0.0)
         o = jnp.dot(w.astype(BF16), value, preferred_element_type=F32)
         total = w if total is None else total + w
         out = o if out is None else out + o
-    return out, top, jnp.sum(total, axis=1, keepdims=True)
+    return out, top * SCALE, jnp.sum(total, axis=1, keepdims=True)
 
 
 def picked_lines(picks, axis):

time: 67.6 us -> 67.3 us (level)
  no operation moved by 1% of the time
where the time goes in v9:
time: 67.3 us; the launch traced here: 67 us
  blocking collectives  49.8 us (74%)
  starting transfers between devices  10.8 us (16%)
  Pallas kernels  6.31 us (9%)
    all_to_all x1, blocking collectives, local(): q = lax.all_to_all(q, PLANE, split_axis=0, concat_axis=0, tiled=True)  30.6 us
    all_to_all x1, blocking collectives, local(): lax.all_to_all(parts, PLANE, split_axis=0, concat_axis=0, tiled=True)  19.2 us
    ppermute x3, starting transfers between devices, turn(): lax.ppermute(value, axis, [(i, (i + step) % size) for i in range(size)])  10.8 us
    pallas_call x1, Pallas kernels, local(): call(pack_kernel, [jax.ShapeDtypeStruct((PEERS, OWN, HEAD_DIM), BF16), ja...  2.75 us
    pallas_call x1, Pallas kernels, local(): call(attend_kernel, jax.ShapeDtypeStruct((PEERS * CHUNK, HEAD_DIM), F32),...  2.67 us
  transfers between devices with their start and end apart: 3, of which 0 were waited for; matrix products, arithmetic and copies ran while one was open for 0% of the time, Pallas kernels for 0%

profile of v9, /device:TPU:1, one launch (start us, length us, event | category | flops | bytes accessed | tf_op | source)
XLA Modules:
  0.0 67.0 jit_solution(1116307033545023185)
XLA Ops:
  0.0 2.8 %shard_map.91 = (bf16[128,4,128]{2,1,0:T(4,128)(2,1)}, bf16[65536,128]{1,0:T(8,128)(2,1)}, bf16[2048,128]{1,0:T(8,128)(2,1)}, bf16[2048,128]{1,0:T(8,128)(2,1)}, bf16[2048,128]{1,0:T(8,128)(2,1)}) custom-call(bf16[1,4,128]{2,1,0:T(4,128)(2,1)} %bitcast.16, s32[64]{0:T(128)} %row_branch.1, s32[4]{0:T(128)} %suffix_len.1, bf16[256,512]{1,0:T(8,128)(2,1)} %ck.1, ...), custom_call_target="tpu_custom_call" | custom-call | tf_op jit(solution)/shard_map/pallas_call | solution.py:274
  2.8 5.5 %collective-permute-start = (bf16[2048,128]{1,0:T(8,128)(2,1)}, bf16[2048,128]{1,0:T(8,128)(2,1)S(1)}, u32[]{:S(2)}, u32[]{:S(2)}) collective-permute-start(bf16[2048,128]{1,0:T(8,128)(2,1)} %get-tuple-element.12), channel_id=1, source_target_pairs={{0,16},{8,24},{16,0},{24,8},{1,17},{9,25},{17,1},{25,9},{2,18},{10... | collective-permute-start | bytes 1572872 | tf_op jit(solution)/shard_map/ppermute | solution.py:253
  8.3 2.8 %collective-permute-start.1 = (bf16[2048,128]{1,0:T(8,128)(2,1)}, bf16[2048,128]{1,0:T(8,128)(2,1)S(1)}, u32[]{:S(2)}, u32[]{:S(2)}) collective-permute-start(bf16[2048,128]{1,0:T(8,128)(2,1)} %get-tuple-element.13), channel_id=1, source_target_pairs={{0,24},{8,0},{16,8},{24,16},{1,25},{9,1},{17,9},{25,17},{2,26},{10... | collective-permute-start | bytes 1572872 | tf_op jit(solution)/shard_map/ppermute | solution.py:253
  11.0 2.5 %collective-permute-start.2 = (bf16[2048,128]{1,0:T(8,128)(2,1)}, bf16[2048,128]{1,0:T(8,128)(2,1)S(1)}, u32[]{:S(2)}, u32[]{:S(2)}) collective-permute-start(bf16[2048,128]{1,0:T(8,128)(2,1)} %get-tuple-element.14), channel_id=1, source_target_pairs={{0,8},{8,16},{16,24},{24,0},{1,9},{9,17},{17,25},{25,1},{2,10},{10... | collective-permute-start | bytes 1572872 | tf_op jit(solution)/shard_map/ppermute | solution.py:253
  13.5 30.6 %all_to_all.10 = bf16[128,4,128]{2,1,0:T(4,128)(2,1)S(1)} all-to-all(bf16[128,4,128]{2,1,0:T(4,128)(2,1)} %get-tuple-element.11), channel_id=1, replica_groups=mesh['ylo'=2,'z'=8,'x'=4,'yhi'=4,'core'=2] {'yhi','ylo','z','core'}, dimensions={0} | all-to-all | bytes 262144 | tf_op jit(solution)/shard_map/all_to_all | solution.py:299
  44.1 0.0 collective-permute-done.kv_a
  44.1 0.0 collective-permute-done.1.kv_b
  44.2 0.0 collective-permute-done.2.kv_c
  44.2 2.7 %shard_map.92 = f32[768,128]{1,0:T(8,128)S(1)} custom-call(bf16[65536,128]{1,0:T(8,128)(2,1)} %get-tuple-element.10.own_hbm, bf16[512,128]{1,0:T(8,128)(2,1)S(1)} %bitcast.9, bf16[2048,128]{1,0:T(8,128)(2,1)S(1)} %collective-permute-done.kv_a, bf16[2048,128]{1,0:T(8,128)(2,1)S(1)} %collective-permute-done.1.kv_b, ...), custom_call_target="tpu_custom_call" | custom-call | tf_op jit(solution)/shard_map/pallas_call | solution.py:301
  46.9 19.2 %all_to_all.11 = f16[384,2,128]{2,1,0:T(2,128)(2,1)S(1)} all-to-all(f16[384,2,128]{2,1,0:T(2,128)(2,1)S(1)} %bitcast.10), channel_id=1, replica_groups=mesh['ylo'=2,'z'=8,'x'=4,'yhi'=4,'core'=2] {'yhi','ylo','z','core'}, dimensions={0} | all-to-all | bytes 393216 | tf_op jit(solution)/shard_map/all_to_all | solution.py:312
  66.1 0.9 %shard_map.93 = bf16[4,128]{1,0:T(4,128)(2,1)} custom-call(f32[768,128]{1,0:T(8,128)S(1)} %convert.1.parts), custom_call_target="tpu_custom_call" | custom-call | tf_op jit(solution)/shard_map/pallas_call | solution.py:314
  (2 shorter events, 0.1 us)
Async XLA Ops:
  2.8 41.4 %collective-permute-start = (bf16[2048,128]{1,0:T(8,128)(2,1)}, bf16[2048,128]{1,0:T(8,128)(2,1)S(1)}, u32[]{:S(2)}, u32[]{:S(2)}) collective-permute-start(bf16[2048,128]{1,0:T(8,128)(2,1)} %get-tuple-element.12), channel_id=1, source_target_pairs={{0,16},{8,24},{16,0},{24,8},{1,17},{9,25},{17,1},{25,9},{2,18},{10... | collective-permute-start | bytes 1572872 | tf_op jit(solution)/shard_map/ppermute | solution.py:253
  8.3 35.9 %collective-permute-start.1 = (bf16[2048,128]{1,0:T(8,128)(2,1)}, bf16[2048,128]{1,0:T(8,128)(2,1)S(1)}, u32[]{:S(2)}, u32[]{:S(2)}) collective-permute-start(bf16[2048,128]{1,0:T(8,128)(2,1)} %get-tuple-element.13), channel_id=1, source_target_pairs={{0,24},{8,0},{16,8},{24,16},{1,25},{9,1},{17,9},{25,17},{2,26},{10... | collective-permute-start | bytes 1572872 | tf_op jit(solution)/shard_map/ppermute | solution.py:253
  11.0 33.1 %collective-permute-start.2 = (bf16[2048,128]{1,0:T(8,128)(2,1)}, bf16[2048,128]{1,0:T(8,128)(2,1)S(1)}, u32[]{:S(2)}, u32[]{:S(2)}) collective-permute-start(bf16[2048,128]{1,0:T(8,128)(2,1)} %get-tuple-element.14), channel_id=1, source_target_pairs={{0,8},{8,16},{16,24},{24,0},{1,9},{9,17},{17,25},{25,1},{2,10},{10... | collective-permute-start | bytes 1572872 | tf_op jit(solution)/shard_map/ppermute | solution.py:253

commit v10 on v9

--- a/solution.py
+++ b/solution.py
@@ -26,7 +26,7 @@
 INFO = 16
 OWN_ROOM = 1 << 16
 CHUNK = OWN + 2
-TOP_AT, TOTAL_AT, POWER_AT = (0, 4, 8), (16, 20, 24), 32
+TOP_AT, TOTAL_AT, POWER_AT = (0, 4, 8), (16, 20), 32
 LOW = -1e30
 F32 = jnp.float32
 BF16 = jnp.bfloat16
@@ -212,7 +212,8 @@
             piece = value.astype(BF16).astype(F32)
             stat = jnp.where(lane == at, piece, stat)
             value = value - piece
-    stat = sum(pltpu.roll(stat, i, 0) for i in range(1, OWN)) + stat
+    stat = stat + pltpu.roll(stat, 1, 0)
+    stat = stat + pltpu.roll(stat, 2, 0)
     for c in range(PEERS):
         out_ref[pl.ds(c * CHUNK, OWN)] = out[c * OWN : (c + 1) * OWN]
         out_ref[pl.ds(c * CHUNK + OWN, 2)] = stat[(c + 1) * OWN - 2 : (c + 1) * OWN]

time: 67.3 us -> 67.2 us (level)
  no operation moved by 1% of the time
where the time goes in v10:
time: 67.2 us; the launch traced here: 66.9 us
  blocking collectives  49.8 us (74%)
  starting transfers between devices  10.8 us (16%)
  Pallas kernels  6.22 us (9%)
    all_to_all x1, blocking collectives, local(): q = lax.all_to_all(q, PLANE, split_axis=0, concat_axis=0, tiled=True)  30.6 us
    all_to_all x1, blocking collectives, local(): lax.all_to_all(parts, PLANE, split_axis=0, concat_axis=0, tiled=True)  19.2 us
    ppermute x3, starting transfers between devices, turn(): lax.ppermute(value, axis, [(i, (i + step) % size) for i in range(size)])  10.8 us
    pallas_call x1, Pallas kernels, local(): call(pack_kernel, [jax.ShapeDtypeStruct((PEERS, OWN, HEAD_DIM), BF16), ja...  2.75 us
    pallas_call x1, Pallas kernels, local(): call(attend_kernel, jax.ShapeDtypeStruct((PEERS * CHUNK, HEAD_DIM), F32),...  2.59 us
  transfers between devices with their start and end apart: 3, of which 0 were waited for; matrix products, arithmetic and copies ran while one was open for 0% of the time, Pallas kernels for 0%

profile of v10, /device:TPU:1, one launch (start us, length us, event | category | flops | bytes accessed | tf_op | source)
XLA Modules:
  0.0 66.9 jit_solution(6771799188294649990)
XLA Ops:
  0.0 2.8 %shard_map.91 = (bf16[128,4,128]{2,1,0:T(4,128)(2,1)}, bf16[65536,128]{1,0:T(8,128)(2,1)}, bf16[2048,128]{1,0:T(8,128)(2,1)}, bf16[2048,128]{1,0:T(8,128)(2,1)}, bf16[2048,128]{1,0:T(8,128)(2,1)}) custom-call(bf16[1,4,128]{2,1,0:T(4,128)(2,1)} %bitcast.16, s32[64]{0:T(128)} %row_branch.1, s32[4]{0:T(128)} %suffix_len.1, bf16[256,512]{1,0:T(8,128)(2,1)} %ck.1, ...), custom_call_target="tpu_custom_call" | custom-call | tf_op jit(solution)/shard_map/pallas_call | solution.py:275
  2.8 5.5 %collective-permute-start = (bf16[2048,128]{1,0:T(8,128)(2,1)}, bf16[2048,128]{1,0:T(8,128)(2,1)S(1)}, u32[]{:S(2)}, u32[]{:S(2)}) collective-permute-start(bf16[2048,128]{1,0:T(8,128)(2,1)} %get-tuple-element.12), channel_id=1, source_target_pairs={{0,16},{8,24},{16,0},{24,8},{1,17},{9,25},{17,1},{25,9},{2,18},{10... | collective-permute-start | bytes 1572872 | tf_op jit(solution)/shard_map/ppermute | solution.py:254
  8.3 2.8 %collective-permute-start.1 = (bf16[2048,128]{1,0:T(8,128)(2,1)}, bf16[2048,128]{1,0:T(8,128)(2,1)S(1)}, u32[]{:S(2)}, u32[]{:S(2)}) collective-permute-start(bf16[2048,128]{1,0:T(8,128)(2,1)} %get-tuple-element.13), channel_id=1, source_target_pairs={{0,24},{8,0},{16,8},{24,16},{1,25},{9,1},{17,9},{25,17},{2,26},{10... | collective-permute-start | bytes 1572872 | tf_op jit(solution)/shard_map/ppermute | solution.py:254
  11.0 2.5 %collective-permute-start.2 = (bf16[2048,128]{1,0:T(8,128)(2,1)}, bf16[2048,128]{1,0:T(8,128)(2,1)S(1)}, u32[]{:S(2)}, u32[]{:S(2)}) collective-permute-start(bf16[2048,128]{1,0:T(8,128)(2,1)} %get-tuple-element.14), channel_id=1, source_target_pairs={{0,8},{8,16},{16,24},{24,0},{1,9},{9,17},{17,25},{25,1},{2,10},{10... | collective-permute-start | bytes 1572872 | tf_op jit(solution)/shard_map/ppermute | solution.py:254
  13.5 30.6 %all_to_all.10 = bf16[128,4,128]{2,1,0:T(4,128)(2,1)S(1)} all-to-all(bf16[128,4,128]{2,1,0:T(4,128)(2,1)} %get-tuple-element.11), channel_id=1, replica_groups=mesh['ylo'=2,'z'=8,'x'=4,'yhi'=4,'core'=2] {'yhi','ylo','z','core'}, dimensions={0} | all-to-all | bytes 262144 | tf_op jit(solution)/shard_map/all_to_all | solution.py:300
  44.1 0.0 collective-permute-done.kv_a
  44.1 0.0 collective-permute-done.1.kv_b
  44.2 0.0 collective-permute-done.2.kv_c
  44.2 2.6 %shard_map.92 = f32[768,128]{1,0:T(8,128)S(1)} custom-call(bf16[65536,128]{1,0:T(8,128)(2,1)} %get-tuple-element.10.own_hbm, bf16[512,128]{1,0:T(8,128)(2,1)S(1)} %bitcast.9, bf16[2048,128]{1,0:T(8,128)(2,1)S(1)} %collective-permute-done.kv_a, bf16[2048,128]{1,0:T(8,128)(2,1)S(1)} %collective-permute-done.1.kv_b, ...), custom_call_target="tpu_custom_call" | custom-call | tf_op jit(solution)/shard_map/pallas_call | solution.py:302
  46.8 19.2 %all_to_all.11 = f16[384,2,128]{2,1,0:T(2,128)(2,1)S(1)} all-to-all(f16[384,2,128]{2,1,0:T(2,128)(2,1)S(1)} %bitcast.10), channel_id=1, replica_groups=mesh['ylo'=2,'z'=8,'x'=4,'yhi'=4,'core'=2] {'yhi','ylo','z','core'}, dimensions={0} | all-to-all | bytes 393216 | tf_op jit(solution)/shard_map/all_to_all | solution.py:313
  66.0 0.9 %shard_map.93 = bf16[4,128]{1,0:T(4,128)(2,1)} custom-call(f32[768,128]{1,0:T(8,128)S(1)} %convert.1.parts), custom_call_target="tpu_custom_call" | custom-call | tf_op jit(solution)/shard_map/pallas_call | solution.py:315
  (2 shorter events, 0.1 us)
Async XLA Ops:
  2.8 41.4 %collective-permute-start = (bf16[2048,128]{1,0:T(8,128)(2,1)}, bf16[2048,128]{1,0:T(8,128)(2,1)S(1)}, u32[]{:S(2)}, u32[]{:S(2)}) collective-permute-start(bf16[2048,128]{1,0:T(8,128)(2,1)} %get-tuple-element.12), channel_id=1, source_target_pairs={{0,16},{8,24},{16,0},{24,8},{1,17},{9,25},{17,1},{25,9},{2,18},{10... | collective-permute-start | bytes 1572872 | tf_op jit(solution)/shard_map/ppermute | solution.py:254
  8.3 35.9 %collective-permute-start.1 = (bf16[2048,128]{1,0:T(8,128)(2,1)}, bf16[2048,128]{1,0:T(8,128)(2,1)S(1)}, u32[]{:S(2)}, u32[]{:S(2)}) collective-permute-start(bf16[2048,128]{1,0:T(8,128)(2,1)} %get-tuple-element.13), channel_id=1, source_target_pairs={{0,24},{8,0},{16,8},{24,16},{1,25},{9,1},{17,9},{25,17},{2,26},{10... | collective-permute-start | bytes 1572872 | tf_op jit(solution)/shard_map/ppermute | solution.py:254
  11.0 33.1 %collective-permute-start.2 = (bf16[2048,128]{1,0:T(8,128)(2,1)}, bf16[2048,128]{1,0:T(8,128)(2,1)S(1)}, u32[]{:S(2)}, u32[]{:S(2)}) collective-permute-start(bf16[2048,128]{1,0:T(8,128)(2,1)} %get-tuple-element.14), channel_id=1, source_target_pairs={{0,8},{8,16},{16,24},{24,0},{1,9},{9,17},{17,25},{25,1},{2,10},{10... | collective-permute-start | bytes 1572872 | tf_op jit(solution)/shard_map/ppermute | solution.py:254

commit v11 on v10

--- a/solution.py
+++ b/solution.py
@@ -14,7 +14,7 @@
 GROUP = HEADS // KV_HEADS
 HEAD_DIM = 128
 N_X, N_YHI, N_CORE, N_YLO, N_Z = 4, 4, 2, 2, 8
-PLANE = ("yhi", "ylo", "z", "core")
+PLANE = ("ylo", "yhi", "z", "core")
 PEERS = N_Z * N_YHI * N_YLO * N_CORE
 STEPS = (2, 3, 1)
 ROWS = 64
@@ -203,15 +203,22 @@
     power = jnp.ceil(jnp.log(jnp.max(jnp.abs(out), axis=1, keepdims=True)) * math.log2(math.e))
     power = jnp.clip(power, -120.0, 120.0)
     out = out * jnp.exp2(-power)
-    shape = (LINES, HEAD_DIM)
-    r = lax.broadcasted_iota(jnp.int32, shape, 0) & (OWN - 1)
-    lane = lax.broadcasted_iota(jnp.int32, shape, 1) - r
-    stat = jnp.where(lane == POWER_AT, power, 0.0)
+    tile = (1, 8, HEAD_DIM)
+    lane = lax.broadcasted_iota(jnp.int32, tile, 2)
+    lane = lane - (lax.broadcasted_iota(jnp.int32, tile, 1) & (OWN - 1))
+    shape = (LINES // 8, 8, HEAD_DIM)
+
+    def lanes_of(at, value):
+        value = jnp.broadcast_to(value, (LINES, HEAD_DIM)).reshape(shape)
+        return jnp.where(jnp.broadcast_to(lane == at, shape), value, 0.0)
+
+    stat = lanes_of(POWER_AT, power)
     for value, lanes in ((high, TOP_AT), (total, TOTAL_AT)):
         for at in lanes:
             piece = value.astype(BF16).astype(F32)
-            stat = jnp.where(lane == at, piece, stat)
+            stat = stat + lanes_of(at, piece)
             value = value - piece
+    stat = stat.reshape(LINES, HEAD_DIM)
     stat = stat + pltpu.roll(stat, 1, 0)
     stat = stat + pltpu.roll(stat, 2, 0)
     for c in range(PEERS):

time: 67.2 us -> 67.3 us (level)
  no operation moved by 1% of the time
where the time goes in v11:
time: 67.3 us; the launch traced here: 67 us
  blocking collectives  49.9 us (74%)
  starting transfers between devices  10.8 us (16%)
  Pallas kernels  6.18 us (9%)
    all_to_all x1, blocking collectives, local(): q = lax.all_to_all(q, PLANE, split_axis=0, concat_axis=0, tiled=True)  31.2 us
    all_to_all x1, blocking collectives, local(): lax.all_to_all(parts, PLANE, split_axis=0, concat_axis=0, tiled=True)  18.7 us
    ppermute x3, starting transfers between devices, turn(): lax.ppermute(value, axis, [(i, (i + step) % size) for i in range(size)])  10.8 us
    pallas_call x1, Pallas kernels, local(): call(pack_kernel, [jax.ShapeDtypeStruct((PEERS, OWN, HEAD_DIM), BF16), ja...  2.75 us
    pallas_call x1, Pallas kernels, local(): call(attend_kernel, jax.ShapeDtypeStruct((PEERS * CHUNK, HEAD_DIM), F32),...  2.56 us
  transfers between devices with their start and end apart: 3, of which 0 were waited for; matrix products, arithmetic and copies ran while one was open for 0% of the time, Pallas kernels for 0%

profile of v11, /device:TPU:1, one launch (start us, length us, event | category | flops | bytes accessed | tf_op | source)
XLA Modules:
  0.0 67.0 jit_solution(13602201762100138180)
XLA Ops:
  0.0 2.8 %shard_map.91 = (bf16[128,4,128]{2,1,0:T(4,128)(2,1)}, bf16[65536,128]{1,0:T(8,128)(2,1)}, bf16[2048,128]{1,0:T(8,128)(2,1)}, bf16[2048,128]{1,0:T(8,128)(2,1)}, bf16[2048,128]{1,0:T(8,128)(2,1)}) custom-call(bf16[1,4,128]{2,1,0:T(4,128)(2,1)} %bitcast.16, s32[64]{0:T(128)} %row_branch.1, s32[4]{0:T(128)} %suffix_len.1, bf16[256,512]{1,0:T(8,128)(2,1)} %ck.1, ...), custom_call_target="tpu_custom_call" | custom-call | tf_op jit(solution)/shard_map/pallas_call | solution.py:282
  2.8 5.5 %collective-permute-start = (bf16[2048,128]{1,0:T(8,128)(2,1)}, bf16[2048,128]{1,0:T(8,128)(2,1)S(1)}, u32[]{:S(2)}, u32[]{:S(2)}) collective-permute-start(bf16[2048,128]{1,0:T(8,128)(2,1)} %get-tuple-element.12), channel_id=1, source_target_pairs={{0,16},{8,24},{16,0},{24,8},{1,17},{9,25},{17,1},{25,9},{2,18},{10... | collective-permute-start | bytes 1572872 | tf_op jit(solution)/shard_map/ppermute | solution.py:261
  8.3 2.8 %collective-permute-start.1 = (bf16[2048,128]{1,0:T(8,128)(2,1)}, bf16[2048,128]{1,0:T(8,128)(2,1)S(1)}, u32[]{:S(2)}, u32[]{:S(2)}) collective-permute-start(bf16[2048,128]{1,0:T(8,128)(2,1)} %get-tuple-element.13), channel_id=1, source_target_pairs={{0,24},{8,0},{16,8},{24,16},{1,25},{9,1},{17,9},{25,17},{2,26},{10... | collective-permute-start | bytes 1572872 | tf_op jit(solution)/shard_map/ppermute | solution.py:261
  11.0 2.5 %collective-permute-start.2 = (bf16[2048,128]{1,0:T(8,128)(2,1)}, bf16[2048,128]{1,0:T(8,128)(2,1)S(1)}, u32[]{:S(2)}, u32[]{:S(2)}) collective-permute-start(bf16[2048,128]{1,0:T(8,128)(2,1)} %get-tuple-element.14), channel_id=1, source_target_pairs={{0,8},{8,16},{16,24},{24,0},{1,9},{9,17},{17,25},{25,1},{2,10},{10... | collective-permute-start | bytes 1572872 | tf_op jit(solution)/shard_map/ppermute | solution.py:261
  13.5 31.2 %all_to_all.10 = bf16[128,4,128]{2,1,0:T(4,128)(2,1)S(1)} all-to-all(bf16[128,4,128]{2,1,0:T(4,128)(2,1)} %get-tuple-element.11), channel_id=1, replica_groups=mesh['ylo'=2,'z'=8,'x'=4,'yhi'=4,'core'=2] {'ylo','yhi','z','core'}, dimensions={0} | all-to-all | bytes 262144 | tf_op jit(solution)/shard_map/all_to_all | solution.py:307
  44.7 0.0 collective-permute-done.kv_a
  44.7 0.0 collective-permute-done.1.kv_b
  44.7 0.0 collective-permute-done.2.kv_c
  44.7 2.6 %shard_map.92 = f32[768,128]{1,0:T(8,128)S(1)} custom-call(bf16[65536,128]{1,0:T(8,128)(2,1)} %get-tuple-element.10.own_hbm, bf16[512,128]{1,0:T(8,128)(2,1)S(1)} %bitcast.9, bf16[2048,128]{1,0:T(8,128)(2,1)S(1)} %collective-permute-done.kv_a, bf16[2048,128]{1,0:T(8,128)(2,1)S(1)} %collective-permute-done.1.kv_b, ...), custom_call_target="tpu_custom_call" | custom-call | tf_op jit(solution)/shard_map/pallas_call | solution.py:309
  47.3 18.7 %all_to_all.11 = f16[384,2,128]{2,1,0:T(2,128)(2,1)S(1)} all-to-all(f16[384,2,128]{2,1,0:T(2,128)(2,1)S(1)} %bitcast.10), channel_id=1, replica_groups=mesh['ylo'=2,'z'=8,'x'=4,'yhi'=4,'core'=2] {'ylo','yhi','z','core'}, dimensions={0} | all-to-all | bytes 393216 | tf_op jit(solution)/shard_map/all_to_all | solution.py:320
  66.1 0.9 %shard_map.93 = bf16[4,128]{1,0:T(4,128)(2,1)} custom-call(f32[768,128]{1,0:T(8,128)S(1)} %convert.1.parts), custom_call_target="tpu_custom_call" | custom-call | tf_op jit(solution)/shard_map/pallas_call | solution.py:322
  (2 shorter events, 0.1 us)
Async XLA Ops:
  2.8 42.0 %collective-permute-start = (bf16[2048,128]{1,0:T(8,128)(2,1)}, bf16[2048,128]{1,0:T(8,128)(2,1)S(1)}, u32[]{:S(2)}, u32[]{:S(2)}) collective-permute-start(bf16[2048,128]{1,0:T(8,128)(2,1)} %get-tuple-element.12), channel_id=1, source_target_pairs={{0,16},{8,24},{16,0},{24,8},{1,17},{9,25},{17,1},{25,9},{2,18},{10... | collective-permute-start | bytes 1572872 | tf_op jit(solution)/shard_map/ppermute | solution.py:261
  8.3 36.5 %collective-permute-start.1 = (bf16[2048,128]{1,0:T(8,128)(2,1)}, bf16[2048,128]{1,0:T(8,128)(2,1)S(1)}, u32[]{:S(2)}, u32[]{:S(2)}) collective-permute-start(bf16[2048,128]{1,0:T(8,128)(2,1)} %get-tuple-element.13), channel_id=1, source_target_pairs={{0,24},{8,0},{16,8},{24,16},{1,25},{9,1},{17,9},{25,17},{2,26},{10... | collective-permute-start | bytes 1572872 | tf_op jit(solution)/shard_map/ppermute | solution.py:261
  11.0 33.7 %collective-permute-start.2 = (bf16[2048,128]{1,0:T(8,128)(2,1)}, bf16[2048,128]{1,0:T(8,128)(2,1)S(1)}, u32[]{:S(2)}, u32[]{:S(2)}) collective-permute-start(bf16[2048,128]{1,0:T(8,128)(2,1)} %get-tuple-element.14), channel_id=1, source_target_pairs={{0,8},{8,16},{16,24},{24,0},{1,9},{9,17},{17,25},{25,1},{2,10},{10... | collective-permute-start | bytes 1572872 | tf_op jit(solution)/shard_map/ppermute | solution.py:261
